TPU v7x, 1024 devices: a whole 4x8x16 slice. The times are simulated.
1024 devices in a mesh: dp: 4 (over z_hi), expert: 8 (over y), tensor: 32 (over x, z_lo, core).
Axes of the slice: x: 4, y: 8, z: 16 (z_hi: 4, z_lo: 4; z = z_hi * 4 + z_lo), core: 2. Of those that a mesh axis runs over, the one named last changes fastest.
Arguments:
- tokens: bfloat16 [4096, 7168], P(('dp', 'expert'), 'tensor'), may hold values from -6 to 6
- cotangent: bfloat16 [4096, 7168], P(('dp', 'expert'), 'tensor'), may hold values from -6 to 6
- route_ids: int32 [4096, 8], P(('dp', 'expert')), may hold values from 0 to 255, all different within a row; in each aligned block of 128 rows (0 to 127, 128 to 255, ...) at most 7 rows name the same one
- gates: float32 [4096, 8], P(('dp', 'expert')), may hold values from 0.2 to 1.2
- w_gate: bfloat16 [16384, 7168], P(('expert', 'tensor')), may hold values from -0.0625 to 0.0625
- w_up: bfloat16 [16384, 7168], P(('expert', 'tensor')), may hold values from -0.0625 to 0.0625
- w_down: bfloat16 [16384, 7168], P(('expert', 'tensor')), may hold values from -0.125 to 0.125
Outputs:
- mixed: bfloat16 [4096, 7168], P(('dp', 'expert'), 'tensor')
- token_grad: bfloat16 [4096, 7168], P(('dp', 'expert'), 'tensor')
- gate_grad: bfloat16 [16384, 7168], P(('expert', 'tensor'), 'dp')
- up_grad: bfloat16 [16384, 7168], P(('expert', 'tensor'), 'dp')
- down_grad: bfloat16 [16384, 7168], P(('expert', 'tensor'), 'dp')
Inputs may be any that keep to these rules, and one draw needn't show every extreme that they name: `route_ids`: each token names 8 different experts. Among the 128 tokens of one block, no expert is named by more than 7 tokens.
All inputs are finite; a program needn't handle non-finite values.
Results may differ from a plain program's by a relative error of at most 0.034.
Values may be sent and summed in bfloat16 or wider, within the bound.
A program may use at most 64 MiB of HBM per device.

v0:
```python
import jax
import jax.numpy as jnp
from jax import lax
from jax.sharding import PartitionSpec as P

EXP_GROUP = 1
CAP = 7


def per_device(tokens, cotangent, route_ids, gates, w_gate, w_up, w_down):
    n_expert = lax.axis_size("expert")
    n_tensor = lax.axis_size("tensor")
    part_cols = tokens.shape[1]
    hid_rows, width = w_gate.shape
    window = EXP_GROUP * n_expert
    copies = n_tensor // EXP_GROUP
    rows_all = n_expert * CAP
    labels = jnp.arange(window, dtype=jnp.int32)
    match = route_ids[:, :, None] == labels[None, None, :]
    hits = jnp.sum(match.astype(jnp.int32), axis=1)
    weight_of = jnp.sum(jnp.where(match, gates[:, :, None], 0.0), axis=1)
    places = jnp.cumsum(hits, axis=0) - 1
    slot_iota = jnp.arange(CAP, dtype=jnp.int32)
    picks = (hits.T[:, None, :] == 1) & (places.T[:, None, :] == slot_iota[None, :, None])
    picker = picks.astype(jnp.bfloat16)
    pick_real = picks.astype(jnp.float32)
    sent_rows = jnp.einsum(
        "wct,td->wcd", picker, tokens, preferred_element_type=jnp.float32
    ).astype(jnp.bfloat16)
    cot_rows = jnp.einsum("wct,td->wcd", picker, cotangent, preferred_element_type=jnp.float32)
    slot_gate = jnp.einsum("wct,tw->wc", pick_real, weight_of, precision=lax.Precision.HIGHEST)
    scaled_rows = (slot_gate[:, :, None] * cot_rows).astype(jnp.bfloat16)
    got_rows, got_cot = (
        lax.all_to_all(sent_rows, "expert", split_axis=0, concat_axis=0, tiled=True),
        lax.all_to_all(scaled_rows, "expert", split_axis=0, concat_axis=0, tiled=True),
    )
    gathered = lax.all_gather(got_rows, "tensor", axis=2, tiled=True)
    gathered = gathered.reshape(n_expert, EXP_GROUP, CAP, width)
    row_full = gathered.reshape(rows_all, width)
    grouped = got_cot.reshape(n_expert, EXP_GROUP, CAP, part_cols).transpose(0, 2, 1, 3)
    grouped = grouped.reshape(rows_all, EXP_GROUP, 1, part_cols)
    wide = jnp.broadcast_to(grouped, (rows_all, EXP_GROUP, copies, part_cols))
    cot_full = lax.all_to_all(
        wide.reshape(rows_all, n_tensor, part_cols),
        "tensor",
        split_axis=1,
        concat_axis=1,
        tiled=True,
    ).reshape(rows_all, width)
    contract_rows = (((0,), (0,)), ((), ()))
    contract_cols = (((1,), (1,)), ((), ()))
    pre = lax.dot_general(row_full, w_gate, contract_cols, preferred_element_type=jnp.float32)
    upper = lax.dot_general(row_full, w_up, contract_cols, preferred_element_type=jnp.float32)
    sig = jax.nn.sigmoid(pre)
    act = pre * sig
    hidden = (act * upper).astype(jnp.bfloat16)
    out_part = jnp.dot(hidden, w_down, preferred_element_type=jnp.float32).astype(jnp.bfloat16)
    down_term = lax.dot_general(hidden, cot_full, contract_rows, preferred_element_type=jnp.float32)
    back = lax.dot_general(cot_full, w_down, contract_cols, preferred_element_type=jnp.float32)
    gate_delta = (back * upper * sig * (1.0 + pre * (1.0 - sig))).astype(jnp.bfloat16)
    up_delta = (back * act).astype(jnp.bfloat16)
    input_part = jnp.dot(gate_delta, w_gate, preferred_element_type=jnp.float32)
    input_part = (input_part + jnp.dot(up_delta, w_up, preferred_element_type=jnp.float32)).astype(
        jnp.bfloat16
    )

    def to_pieces(full):
        return full.reshape(rows_all, n_tensor, part_cols)

    back_out, back_input = (
        lax.all_to_all(to_pieces(out_part), "tensor", split_axis=1, concat_axis=1, tiled=True),
        lax.all_to_all(to_pieces(input_part), "tensor", split_axis=1, concat_axis=1, tiled=True),
    )

    def settle(pieces):
        summed = jnp.sum(
            pieces.astype(jnp.float32).reshape(rows_all, EXP_GROUP, copies, part_cols), axis=2
        )
        summed = summed.astype(jnp.bfloat16).reshape(n_expert, CAP, EXP_GROUP, part_cols)
        return summed.transpose(0, 2, 1, 3).reshape(window, CAP, part_cols)

    gate_term = lax.dot_general(
        gate_delta, row_full, contract_rows, preferred_element_type=jnp.float32
    )
    up_term = lax.dot_general(up_delta, row_full, contract_rows, preferred_element_type=jnp.float32)
    ret_out, ret_input = (
        lax.all_to_all(settle(back_out), "expert", split_axis=0, concat_axis=0, tiled=True),
        lax.all_to_all(settle(back_input), "expert", split_axis=0, concat_axis=0, tiled=True),
    )
    gate_share, up_share, down_share = (
        lax.psum_scatter(
            gate_term.astype(jnp.bfloat16), "dp", scatter_dimension=1, tiled=True
        ).astype(jnp.float32),
        lax.psum_scatter(
            up_term.astype(jnp.bfloat16), "dp", scatter_dimension=1, tiled=True
        ).astype(jnp.float32),
        lax.psum_scatter(
            down_term.astype(jnp.bfloat16), "dp", scatter_dimension=1, tiled=True
        ).astype(jnp.float32),
    )
    expanded = jnp.einsum("wct,wcd->wtd", picker, ret_out, preferred_element_type=jnp.float32)
    mixed = jnp.sum(weight_of.T[:, :, None] * expanded, axis=0).astype(jnp.bfloat16)
    token_grad = jnp.einsum(
        "wct,wcd->td", picker, ret_input, preferred_element_type=jnp.float32
    ).astype(jnp.bfloat16)
    return (
        mixed,
        token_grad,
        gate_share.astype(jnp.bfloat16),
        up_share.astype(jnp.bfloat16),
        down_share.astype(jnp.bfloat16),
    )


def solution(mesh):
    in_specs = (
        P(("dp", "expert"), "tensor"),
        P(("dp", "expert"), "tensor"),
        P(("dp", "expert"), None),
        P(("dp", "expert"), None),
        P(("expert", "tensor"), None),
        P(("expert", "tensor"), None),
        P(("expert", "tensor"), None),
    )
    out_specs = (
        P(("dp", "expert"), "tensor"),
        P(("dp", "expert"), "tensor"),
        P(("expert", "tensor"), "dp"),
        P(("expert", "tensor"), "dp"),
        P(("expert", "tensor"), "dp"),
    )
    return jax.shard_map(
        per_device, mesh=mesh, in_specs=in_specs, out_specs=out_specs, check_vma=False
    )
```

profile of v0, /device:TPU:1, one launch (start us, length us, event | category | flops | bytes accessed | tf_op | source)
XLA Modules:
  0.0 478.8 jit_solution(1491577834547733842)
XLA Ops:
  7.2 0.0 copy-start
  7.2 0.8 convert_reduce_fusion
  8.0 0.1 copy.50
  8.1 0.2 reduce_window_sum.11
  8.3 0.7 select_reduce_fusion
  9.1 0.6 copy-done.11
  9.7 0.2 fusion.9
  9.8 0.1 copy.62
  9.9 1.0 fusion.3
  10.9 0.7 copy.57
  11.5 7.7 %all-to-all-start.3 = ((bf16[8,7,224]{2,1,0:T(8,128)(2,1)}), bf16[8,7,224]{2,1,0:T(8,128)(2,1)S(1)}, u32[]{:S(2)}, u32[]{:S(2)}) async-start(bf16[8,7,224]{2,1,0:T(8,128)(2,1)} %copy.57), calls=%async_computation.3 | async-start | bytes 65536 | tf_op jit(solution)/shard_map/all_to_all | solution.py:35
  19.2 1.0 convolution_convert_fusion.4
  20.2 0.7 copy.52
  20.8 5.3 %all-to-all-done.3 = bf16[8,7,224]{2,1,0:T(8,128)(2,1)S(1)} async-done(((bf16[8,7,224]{2,1,0:T(8,128)(2,1)}), bf16[8,7,224]{2,1,0:T(8,128)(2,1)S(1)}, u32[]{:S(2)}, u32[]{:S(2)}) %all-to-all-start.3) | async-done | bytes 25120 | tf_op jit(solution)/shard_map/all_to_all | solution.py:35
  26.1 3.3 all-to-all-start
  29.5 7.0 %all-to-all-done = bf16[8,7,224]{2,1,0:T(8,128)(2,1)S(1)} async-done(((bf16[8,7,224]{2,1,0:T(8,128)(2,1)}), bf16[8,7,224]{2,1,0:T(8,128)(2,1)S(1)}, u32[]{:S(2)}, u32[]{:S(2)}) %all-to-all-start) | async-done | bytes 25120 | tf_op jit(solution)/shard_map/all_to_all | solution.py:34
  36.5 1.0 reshape.47
  37.5 15.6 %all-to-all-start.4 = ((bf16[56,32,224]{2,0,1:T(8,128)(2,1)}), bf16[56,32,224]{2,0,1:T(8,128)(2,1)S(1)}, u32[]{:S(2)}, u32[]{:S(2)}) async-start(bf16[56,32,224]{2,0,1:T(8,128)(2,1)} %reshape.47), calls=%async_computation.4 | async-start | bytes 1835008 | tf_op jit(solution)/shard_map/all_to_all | solution.py:43
  53.2 0.3 copy.53
  53.5 192.9 %all_gather.3 = bf16[8,7,7168]{1,0,2:T(8,128)(2,1)} all-gather(bf16[8,7,224]{1,0,2:T(8,128)(2,1)S(1)} %copy.53), channel_id=1, replica_groups=mesh['dp'=4,'expert'=8,'tensor'=32] {'tensor'}, dimensions={2}, use_global_device_ids=true | all-gather | bytes 827904 | tf_op jit(solution)/shard_map/all_gather | solution.py:37
  246.4 15.4 %copy.54 = bf16[8,7,7168]{2,1,0:T(8,128)(2,1)} copy(bf16[8,7,7168]{1,0,2:T(8,128)(2,1)} %all_gather.3) | data formatting | bytes 1605632 | tf_op jit(solution)/shard_map/all_gather | solution.py:37
  261.8 1.5 reshape_reshape.3
  263.3 0.0 copy-start.1
  263.3 1.6 fusion.15
  265.0 0.4 fusion.16
  265.4 1.1 copy.58
  266.5 2.4 reshape.48
  269.0 0.4 multiply_convert_fusion
  269.4 0.0 copy-start.3
  269.4 0.0 copy-start.4
  269.4 0.6 copy-done.3
  270.0 1.3 convolution_convert_fusion.3
  271.2 2.5 reshape.46
  273.7 1.5 copy.55
  275.2 3.7 all-to-all-start.1
  278.9 0.0 reduce-scatter.4.cloned.1.call-start
  278.9 1.4 convolution_convert_fusion.2
  280.3 0.0 reduce-scatter.4.cloned.1.call-update
  280.3 0.2 reduce-scatter.6.cloned.1.call-start
  280.6 1.4 convolution_convert_fusion.1
  282.0 0.0 reduce-scatter.6.cloned.1.call-update
  282.0 0.0 copy-start.5
  282.0 1.6 fusion.17
  283.7 1.3 fusion
  284.9 2.5 reshape.49
  287.4 1.4 copy.59
  288.8 15.3 %all-to-all-done.1 = bf16[56,32,224]{2,0,1:T(8,128)(2,1)S(1)} async-done(((bf16[56,32,224]{2,0,1:T(8,128)(2,1)}), bf16[56,32,224]{2,0,1:T(8,128)(2,1)S(1)}, u32[]{:S(2)}, u32[]{:S(2)}) %all-to-all-start.1) | async-done | bytes 802848 | tf_op jit(solution)/shard_map/all_to_all | solution.py:71
  304.1 3.9 all-to-all-start.5
  308.0 0.0 reduce-scatter.8.cloned.1.call-start
  308.0 2.1 convolution_convert_fusion
  310.1 0.0 reduce-scatter.8.cloned.1.call-update
  310.1 0.2 reduce_sum.53
  310.3 0.6 convert_element_type.67
  310.9 44.3 %all-to-all-done.5 = bf16[56,32,224]{2,0,1:T(8,128)(2,1)S(1)} async-done(((bf16[56,32,224]{2,0,1:T(8,128)(2,1)}), bf16[56,32,224]{2,0,1:T(8,128)(2,1)S(1)}, u32[]{:S(2)}, u32[]{:S(2)}) %all-to-all-start.5) | async-done | bytes 802848 | tf_op jit(solution)/shard_map/all_to_all | solution.py:72
  355.2 5.3 %all-to-all-start.2 = ((bf16[8,7,224]{2,1,0:T(8,128)(2,1)}), bf16[8,7,224]{2,1,0:T(8,128)(2,1)S(1)}, u32[]{:S(2)}, u32[]{:S(2)}) async-start(bf16[8,7,224]{2,1,0:T(8,128)(2,1)} %convert_element_type.67), calls=%async_computation.2 | async-start | bytes 65536 | tf_op jit(solution)/shard_map/all_to_all | solution.py:87
  360.6 0.2 reduce_sum.55
  360.7 0.6 convert_element_type.73
  361.4 6.1 %all-to-all-done.2 = bf16[8,7,224]{2,1,0:T(8,128)(2,1)S(1)} async-done(((bf16[8,7,224]{2,1,0:T(8,128)(2,1)}), bf16[8,7,224]{2,1,0:T(8,128)(2,1)S(1)}, u32[]{:S(2)}, u32[]{:S(2)}) %all-to-all-start.2) | async-done | bytes 25120 | tf_op jit(solution)/shard_map/all_to_all | solution.py:87
  367.4 3.3 all-to-all-start.6
  370.8 1.0 fusion.1
  371.8 5.9 %all-to-all-done.6 = bf16[8,7,224]{2,1,0:T(8,128)(2,1)S(1)} async-done(((bf16[8,7,224]{2,1,0:T(8,128)(2,1)}), bf16[8,7,224]{2,1,0:T(8,128)(2,1)S(1)}, u32[]{:S(2)}, u32[]{:S(2)}) %all-to-all-start.6) | async-done | bytes 25120 | tf_op jit(solution)/shard_map/all_to_all | solution.py:88
  377.6 0.9 fusion.2
  378.5 36.3 %reduce-scatter.6.cloned.1.call-done = bf16[64,1792]{1,0:T(8,128)(2,1)} async-done(((bf16[64,7168]{1,0:T(8,128)(2,1)}), bf16[64,1792]{1,0:T(8,128)(2,1)}) %reduce-scatter.6.cloned.1.call-update) | async-done | bytes 229392 | tf_op jit(solution)/shard_map/reduce_scatter | solution.py:94
  414.8 57.5 %reduce-scatter.8.cloned.1.call-done = bf16[64,1792]{1,0:T(8,128)(2,1)} async-done(((bf16[64,7168]{1,0:T(8,128)(2,1)}), bf16[64,1792]{1,0:T(8,128)(2,1)}) %reduce-scatter.8.cloned.1.call-update) | async-done | bytes 229392 | tf_op jit(solution)/shard_map/reduce_scatter | solution.py:97
  (30 shorter events, 0.1 us)
Async XLA Ops:
  7.2 261.8 %copy-start = (bf16[64,7168]{1,0:T(8,128)(2,1)S(1)}, bf16[64,7168]{1,0:T(8,128)(2,1)}, u32[]{:S(2)}) copy-start(bf16[64,7168]{1,0:T(8,128)(2,1)} %param.13) | copy-start | bytes 2752516
  8.1 29.4 %copy-start.9 = (pred[8,128]{1,0:T(8,128)(4,1)}, pred[8,128]{1,0:T(8,128)(4,1)S(1)}, u32[]{:S(2)}) copy-start(pred[8,128]{1,0:T(8,128)(4,1)S(1)} %compare_bitcast_fusion) | copy-start | bytes 3076
  8.3 29.2 %copy-start.7 = (s32[8,128]{1,0:T(8,128)}, s32[8,128]{1,0:T(8,128)S(1)}, u32[]{:S(2)}) copy-start(s32[8,128]{1,0:T(8,128)S(1)} %copy.51) | copy-start | bytes 12292
  9.1 28.5 %copy-start.13 = (f32[128,8]{0,1:T(8,128)}, f32[128,8]{0,1:T(8,128)S(1)}, u32[]{:S(2)}) copy-start(f32[128,8]{0,1:T(8,128)S(1)} %select_reduce_fusion) | copy-start | bytes 12292
  9.1 0.6 copy-start.11
  11.5 14.5 %all-to-all-start.3 = ((bf16[8,7,224]{2,1,0:T(8,128)(2,1)}), bf16[8,7,224]{2,1,0:T(8,128)(2,1)S(1)}, u32[]{:S(2)}, u32[]{:S(2)}) async-start(bf16[8,7,224]{2,1,0:T(8,128)(2,1)} %copy.57), calls=%async_computation.3 | async-start | bytes 65536 | tf_op jit(solution)/shard_map/all_to_all | solution.py:35
  26.1 10.4 %all-to-all-start = ((bf16[8,7,224]{2,1,0:T(8,128)(2,1)}), bf16[8,7,224]{2,1,0:T(8,128)(2,1)S(1)}, u32[]{:S(2)}, u32[]{:S(2)}) async-start(bf16[8,7,224]{2,1,0:T(8,128)(2,1)} %copy.52), calls=%async_computation | async-start | bytes 65536 | tf_op jit(solution)/shard_map/all_to_all | solution.py:34
  37.5 227.9 %all-to-all-start.4 = ((bf16[56,32,224]{2,0,1:T(8,128)(2,1)}), bf16[56,32,224]{2,0,1:T(8,128)(2,1)S(1)}, u32[]{:S(2)}, u32[]{:S(2)}) async-start(bf16[56,32,224]{2,0,1:T(8,128)(2,1)} %reshape.47), calls=%async_computation.4 | async-start | bytes 1835008 | tf_op jit(solution)/shard_map/all_to_all | solution.py:43
  263.3 1.7 copy-start.1
  269.4 0.6 copy-start.3
  269.4 9.5 %copy-start.6 = (bf16[56,64]{1,0:T(8,128)(2,1)}, bf16[56,64]{1,0:T(8,128)(2,1)S(1)}, u32[]{:S(2)}) copy-start(bf16[56,64]{1,0:T(8,128)(2,1)S(1)} %get-tuple-element.6) | copy-start | bytes 21508
  269.4 11.2 %copy-start.4 = (bf16[56,64]{1,0:T(8,128)(2,1)}, bf16[56,64]{1,0:T(8,128)(2,1)S(1)}, u32[]{:S(2)}) copy-start(bf16[56,64]{1,0:T(8,128)(2,1)S(1)} %get-tuple-element.5) | copy-start | bytes 21508
  275.2 28.9 %all-to-all-start.1 = ((bf16[56,32,224]{2,0,1:T(8,128)(2,1)}), bf16[56,32,224]{2,0,1:T(8,128)(2,1)S(1)}, u32[]{:S(2)}, u32[]{:S(2)}) async-start(bf16[56,32,224]{2,0,1:T(8,128)(2,1)} %copy.55), calls=%async_computation.1 | async-start | bytes 1835008 | tf_op jit(solution)/shard_map/all_to_all | solution.py:71
  278.9 99.6 %reduce-scatter.4.cloned.1.call-start = ((), (), s32[]{:S(2)}) async-start(), calls=%async_computation.10 | async-start | bytes 1146880 | tf_op jit(solution)/shard_map/reduce_scatter | solution.py:91
  280.3 134.4 %reduce-scatter.6.cloned.1.call-start = ((), (), s32[]{:S(2)}) async-start(), calls=%async_computation.11 | async-start | bytes 1146880 | tf_op jit(solution)/shard_map/reduce_scatter | solution.py:94
  282.0 1.7 copy-start.2
  282.0 1.7 copy-start.5
  304.1 51.1 %all-to-all-start.5 = ((bf16[56,32,224]{2,0,1:T(8,128)(2,1)}), bf16[56,32,224]{2,0,1:T(8,128)(2,1)S(1)}, u32[]{:S(2)}, u32[]{:S(2)}) async-start(bf16[56,32,224]{2,0,1:T(8,128)(2,1)} %copy.59), calls=%async_computation.5 | async-start | bytes 1835008 | tf_op jit(solution)/shard_map/all_to_all | solution.py:72
  308.0 164.3 %reduce-scatter.8.cloned.1.call-start = ((), (), s32[]{:S(2)}) async-start(), calls=%async_computation.12 | async-start | bytes 1146880 | tf_op jit(solution)/shard_map/reduce_scatter | solution.py:97
  310.1 60.7 %copy-start.12 = (pred[8,7,128]{2,0,1:T(8,128)(4,1)S(1)}, pred[8,7,128]{2,0,1:T(8,128)(4,1)}, u32[]{:S(2)}) copy-start(pred[8,7,128]{2,0,1:T(8,128)(4,1)} %copy-done.11) | copy-start | bytes 21508
  310.1 60.7 %copy-start.14 = (f32[128,8]{0,1:T(8,128)S(1)}, f32[128,8]{0,1:T(8,128)}, u32[]{:S(2)}) copy-start(f32[128,8]{0,1:T(8,128)} %copy-done.13) | copy-start | bytes 12292
  310.1 67.5 %copy-start.8 = (s32[8,128]{1,0:T(8,128)S(1)}, s32[8,128]{1,0:T(8,128)}, u32[]{:S(2)}) copy-start(s32[8,128]{1,0:T(8,128)} %copy-done.7) | copy-start | bytes 12292
  310.1 67.5 %copy-start.10 = (pred[8,128]{1,0:T(8,128)(4,1)S(1)}, pred[8,128]{1,0:T(8,128)(4,1)}, u32[]{:S(2)}) copy-start(pred[8,128]{1,0:T(8,128)(4,1)} %copy-done.9) | copy-start | bytes 3076
  355.2 12.2 %all-to-all-start.2 = ((bf16[8,7,224]{2,1,0:T(8,128)(2,1)}), bf16[8,7,224]{2,1,0:T(8,128)(2,1)S(1)}, u32[]{:S(2)}, u32[]{:S(2)}) async-start(bf16[8,7,224]{2,1,0:T(8,128)(2,1)} %convert_element_type.67), calls=%async_computation.2 | async-start | bytes 65536 | tf_op jit(solution)/shard_map/all_to_all | solution.py:87
  367.4 10.2 %all-to-all-start.6 = ((bf16[8,7,224]{2,1,0:T(8,128)(2,1)}), bf16[8,7,224]{2,1,0:T(8,128)(2,1)S(1)}, u32[]{:S(2)}, u32[]{:S(2)}) async-start(bf16[8,7,224]{2,1,0:T(8,128)(2,1)} %convert_element_type.73), calls=%async_computation.6 | async-start | bytes 65536 | tf_op jit(solution)/shard_map/all_to_all | solution.py:88
Sparse Core Ops, SparseCore 0:
  283.7 53.5 reduce-scatter.3
  341.4 73.3 reduce-scatter.5
  418.8 53.4 reduce-scatter.7
where the time goes:
time: 480 us; the launch traced here: 479 us
  blocking collectives  193 us (40%)
  waiting for transfers between devices  178 us (37%)
  starting transfers between devices  43.2 us (9%)
  local copies, waits for them, and re-layouts  33.7 us (7%)
  matrix products  15.3 us (3%)
  between operations  14 us (3%)
    all_gather x1, blocking collectives, per_device(): gathered = lax.all_gather(got_rows, 'tensor', axis=2, tiled=True)  193 us
    reduce_scatter x1, waiting for transfers between devices, per_device(): lax.psum_scatter(down_term.astype(jnp.bfloat16), 'dp', scatter_dimension=...  57.5 us
    all_to_all x1, waiting for transfers between devices, per_device(): lax.all_to_all(to_pieces(input_part), 'tensor', split_axis=1, concat_axis...  44.3 us
    reduce_scatter x1, waiting for transfers between devices, per_device(): lax.psum_scatter(up_term.astype(jnp.bfloat16), 'dp', scatter_dimension=1,...  36.3 us
    all_to_all x1, starting transfers between devices, per_device(): lax.all_to_all(wide.reshape(rows_all, n_tensor, part_cols), 'tensor', spl...  15.6 us
    all_gather x1, local copies, waits for them, and re-layouts, per_device(): gathered = lax.all_gather(got_rows, 'tensor', axis=2, tiled=True)  15.4 us
    all_to_all x1, waiting for transfers between devices, per_device(): lax.all_to_all(to_pieces(out_part), 'tensor', split_axis=1, concat_axis=1...  15.3 us
  transfers between devices with their start and end apart: 10, of which 8 were waited for; matrix products, arithmetic and copies ran while one was open for 8% of the time, Pallas kernels for 0%

commit v1 on v0

v1 whole, which is shorter than its diff:
```python
import jax
import jax.numpy as jnp
from jax import lax
from jax.experimental import pallas as pl
from jax.experimental.pallas import tpu as pltpu
from jax.sharding import PartitionSpec as P

NX, NZ, NC = 4, 4, 2
NY = 8
NDP = 4
CHUNKS = NX * NZ * NC
BLK = 16
ROWS = NY * BLK
HALF = ROWS // 2
QUART = ROWS // 4
LANES = 256
HID = 64
N_SEMS = 208
BF16 = jnp.bfloat16
F32 = jnp.float32


def wrap(value, size):
    return lax.rem(value, size)


def nt_dot(left, right):
    return lax.dot_general(left, right, (((1,), (1,)), ((), ())), preferred_element_type=F32)


def kernel(
    tok, cot, rid, gat, wg, wu, wd,
    mixed, tgrad, ggrad, ugrad, dgrad,
    wraw, wt, disp, chunk, acc, mine, compact,
    extra, part, kept, sib_in, opp_out, opp_a, opp_b, right_out, left_out,
    from_left, from_right, z_out, z_in, total, ret_out, ret, gbuf, sems,
):
    dp = lax.axis_index("dp")
    y = lax.axis_index("expert")
    t = lax.axis_index("tensor")
    x = t // (NZ * NC)
    z = wrap(t // NC, NZ)
    c = wrap(t, NC)
    other = 1 - c
    xr, xl, xo = wrap(x + 1, NX), wrap(x + 3, NX), wrap(x + 2, NX)
    cols = tok.shape[1]
    count = [0]

    def take(n=1):
        base = count[0]
        count[0] += n
        assert count[0] <= N_SEMS
        return base

    def tensor_at(x_, z_, c_):
        return {"tensor": x_ * (NZ * NC) + z_ * NC + c_}

    def at(c_, x_, z_):
        return c_ * (NX * NZ) + x_ * NZ + z_

    sibling = tensor_at(x, z, other)
    right, left = tensor_at(xr, z, c), tensor_at(xl, z, c)

    def z_peer(k):
        return tensor_at(x, wrap(z + k, NZ), c)

    def y_peer(k):
        return {"expert": wrap(y + k, NY)}

    def dp_peer(k):
        return {"dp": wrap(dp + k, NDP)}

    barrier = pltpu.get_barrier_semaphore()
    partners = [y_peer(k) for k in range(1, NY)]
    partners += [z_peer(k) for k in range(1, NZ)]
    partners += [dp_peer(k) for k in range(1, NDP)]
    partners += [sibling, right, left]
    for where in partners:
        pl.semaphore_signal(barrier, inc=1, device_id=where, device_id_type=pl.DeviceIdType.MESH)

    def send(src, dst, recv, where):
        copy = pltpu.make_async_remote_copy(
            src_ref=src, dst_ref=dst, send_sem=sems.at[take()], recv_sem=sems.at[recv],
            device_id=where, device_id_type=pl.DeviceIdType.MESH,
        )
        copy.start()
        return copy

    def arrived(ref, sem):
        pltpu.make_async_copy(ref, ref, sems.at[sem]).wait()

    loads = []
    for i, ref in enumerate((wg, wu, wd)):
        copy = pltpu.make_async_copy(ref, wraw.at[i], sems.at[take()])
        copy.start()
        loads.append(copy)

    lane = lax.broadcasted_iota(jnp.int32, (ROWS, ROWS), 1)
    row = lax.broadcasted_iota(jnp.int32, (ROWS, ROWS), 0)
    label = lane // BLK
    routes, weights = rid[...], gat[...]
    hits = jnp.zeros((ROWS, ROWS), F32)
    weight_of = jnp.zeros((ROWS, ROWS), F32)
    for k in range(routes.shape[1]):
        same = routes[:, k : k + 1] == label
        hits = hits + jnp.where(same, 1.0, 0.0)
        weight_of = weight_of + jnp.where(same, weights[:, k : k + 1], 0.0)
    lower = jnp.where(lane <= row, 1.0, 0.0).astype(BF16)
    places = jnp.dot(lower, hits.astype(BF16), preferred_element_type=F32) - 1.0
    slot = wrap(lane, BLK // 2).astype(F32)
    pick = jnp.where((hits == 1.0) & (places == slot), 1.0, 0.0)
    first_lane = wrap(lane // (BLK // 2), 2) == 0
    first_row = wrap(row // (BLK // 2), 2) == 0
    pick_t = jnp.transpose(pick)
    slot_gate = jnp.sum(jnp.transpose(pick * weight_of), axis=1, keepdims=True)
    pick_tok = jnp.where(first_row, pick_t, 0.0).astype(BF16)
    pick_cot = jnp.where(first_row, 0.0, pick_t).astype(BF16)
    rows_tok = jnp.dot(pick_tok, tok[...], preferred_element_type=F32)
    rows_cot = jnp.dot(pick_cot, cot[...], preferred_element_type=F32)
    disp[...] = jnp.zeros_like(disp)
    disp[:, 0:cols] = (rows_tok + slot_gate * rows_cot).astype(BF16)

    pl.semaphore_wait(barrier, len(partners))

    me = at(c, x, z)
    my_rows = pl.ds(pl.multiple_of(y * BLK, BLK), BLK)
    sent_y = []
    y_in = take(NY - 1)
    for k in range(1, NY):
        there = pl.ds(pl.multiple_of(wrap(y + k, NY) * BLK, BLK), BLK)
        sent_y.append(send(disp.at[there], chunk.at[me, my_rows], y_in + k - 1, y_peer(k)))
    chunk[me, my_rows, :] = disp[my_rows, :]

    for copy in loads:
        copy.wait()
    wt[:, :, LANES // 2 :] = jnp.zeros((CHUNKS, LANES, LANES // 2), BF16)
    wt[:, 3 * HID :, : LANES // 2] = jnp.zeros((CHUNKS, LANES - 3 * HID, LANES // 2), BF16)
    for tt in range(CHUNKS):
        g = at(tt % NC, tt // (NZ * NC), (tt // NC) % NZ)
        for i in range(3):
            wt[g, HID * i : HID * (i + 1), 0:cols] = wraw[i, :, cols * tt : cols * (tt + 1)]
    acc[...] = jnp.zeros_like(acc)

    for k in range(1, NY):
        from_y = pl.ds(pl.multiple_of(wrap(y + NY - k, NY) * BLK, BLK), BLK)
        arrived(chunk.at[me, from_y], y_in + k - 1)

    def consume(g):
        acc[...] += nt_dot(chunk[g], wt[g])

    sib_sem = take(NX * NZ)
    z_sem = take(NZ - 1)
    left_sem, right_sem = take(NZ), take(NZ)
    oa_sem, ob_sem = take(NZ), take(NZ)
    sent_g = []

    def to_sibling(x_, z_):
        g = at(c, x_, z_)
        sent_g.append(send(chunk.at[g], chunk.at[g], sib_sem + x_ * NZ + z_, sibling))

    def z_at(k):
        return wrap(z + NZ - k, NZ)

    for k in range(NZ):
        zk = z_at(k)
        g = at(c, x, zk)
        if k > 0:
            arrived(chunk.at[g], z_sem + k - 1)
        sent_g.append(send(chunk.at[g], chunk.at[g], left_sem + zk, right))
        sent_g.append(send(chunk.at[g], chunk.at[g], right_sem + zk, left))
        if k == 0:
            for j in range(1, NZ):
                sent_g.append(send(chunk.at[g], chunk.at[g], z_sem + j - 1, z_peer(j)))
        to_sibling(x, zk)
        consume(g)
    for k in range(NZ):
        zk = z_at(k)
        g = at(c, xl, zk)
        half = (g, pl.ds(0, HALF))
        arrived(chunk.at[g], left_sem + zk)
        sent_g.append(send(chunk.at[half], chunk.at[half], oa_sem + zk, right))
        to_sibling(xl, zk)
        consume(g)
        g = at(c, xr, zk)
        half = (g, pl.ds(HALF, HALF))
        arrived(chunk.at[g], right_sem + zk)
        sent_g.append(send(chunk.at[half], chunk.at[half], ob_sem + zk, left))
        to_sibling(xr, zk)
        consume(g)
    for k in range(NZ):
        zk = z_at(k)
        g = at(c, xo, zk)
        arrived(chunk.at[g, pl.ds(0, HALF)], oa_sem + zk)
        arrived(chunk.at[g, pl.ds(HALF, HALF)], ob_sem + zk)
        to_sibling(xo, zk)
        consume(g)

    quarter = pl.ds(pl.multiple_of(x * QUART, QUART), QUART)
    q_sem = take(NDP - 1)
    sent_q = []
    for k in range(1, NDP):
        src = chunk.at[at(c, wrap(dp + k, NDP), z), quarter]
        sent_q.append(send(src, extra.at[k - 1, c * NZ + z, quarter], q_sem + k - 1, dp_peer(k)))

    for x_ in (x, xl, xr, xo):
        for k in range(NZ):
            zk = z_at(k)
            g = at(other, x_, zk)
            arrived(chunk.at[g], sib_sem + x_ * NZ + zk)
            consume(g)

    whole = acc[...].reshape(NY, 2, BLK // 2, LANES)
    half_rows = NY * BLK // 2
    fwd = whole[:, 0].reshape(half_rows, LANES)[:, : 2 * HID]
    bwd = whole[:, 1].reshape(half_rows, LANES)[:, 2 * HID :]
    low = lax.broadcasted_iota(jnp.int32, (half_rows, 2 * HID), 1) < HID
    turned = pltpu.roll(fwd, HID, 1)
    pre = jnp.where(low, fwd, turned)
    upper = jnp.where(low, turned, fwd)
    back = bwd + pltpu.roll(bwd, HID, 1)
    sig = jax.nn.sigmoid(pre)
    act = pre * sig
    hidden = act * upper
    gate_delta = back * upper * sig * (1.0 + pre * (1.0 - sig))
    up_delta = back * act
    deltas = jnp.where(low, gate_delta, up_delta)
    hid = jnp.where(low, hidden, 0.0)
    compact[NDP - 1] = jnp.concatenate([deltas, hid], axis=1).astype(BF16)
    zeros = jnp.zeros((NY, BLK // 2, 2 * HID), F32)
    top = jnp.concatenate([zeros, hid.reshape(NY, BLK // 2, 2 * HID)], axis=2)
    bottom = jnp.concatenate([deltas.reshape(NY, BLK // 2, 2 * HID), zeros], axis=2)
    mine[...] = jnp.concatenate([top, bottom], axis=1).reshape(ROWS, LANES).astype(BF16)

    m_sem = take(NDP - 1)
    sent_m = []
    for k in range(1, NDP):
        sent_m.append(send(compact.at[NDP - 1], compact.at[k - 1], m_sem + k - 1, dp_peer(k)))

    sr_sem = take(NZ)
    xa_sem, xb_sem = take(NZ), take(NZ)
    nl_sem, nr_sem = take(NZ), take(NZ)
    zr_sem = take(NZ - 1)
    sent_r = []

    def stage_a(k):
        zk = wrap(z + k + 1, NZ)
        left_side = mine[...]

        def one(x_, carry):
            part[k, x_] = jnp.dot(
                left_side, wt[at(other, x_, zk)], preferred_element_type=F32
            ).astype(BF16)
            return carry

        lax.fori_loop(0, NX, one, 0)
        sent_r.append(send(part.at[k], sib_in.at[k], sr_sem + k, sibling))

        def two(x_, carry):
            kept[k, x_] = jnp.dot(left_side, wt[at(c, x_, zk)], preferred_element_type=F32)
            return carry

        lax.fori_loop(0, NX, two, 0)

    def pair(k, x_):
        return kept[k, x_] + sib_in[k, x_].astype(F32)

    def stage_b(k):
        arrived(sib_in.at[k], sr_sem + k)
        opp_out[k] = pair(k, xo).astype(BF16)
        sent_r.append(send(opp_out.at[k, pl.ds(0, HALF)], opp_a.at[k], xa_sem + k, right))
        sent_r.append(send(opp_out.at[k, pl.ds(HALF, HALF)], opp_b.at[k], xb_sem + k, left))

    def stage_c(k):
        arrived(opp_a.at[k], xa_sem + k)
        value = pair(k, xr)
        right_out[k, :HALF] = (value[:HALF] + opp_a[k].astype(F32)).astype(BF16)
        right_out[k, HALF:] = value[HALF:].astype(BF16)
        sent_r.append(send(right_out.at[k], from_left.at[k], nl_sem + k, right))
        arrived(opp_b.at[k], xb_sem + k)
        value = pair(k, xl)
        left_out[k, :HALF] = value[:HALF].astype(BF16)
        left_out[k, HALF:] = (value[HALF:] + opp_b[k].astype(F32)).astype(BF16)
        sent_r.append(send(left_out.at[k], from_right.at[k], nr_sem + k, left))

    def stage_d(k):
        arrived(from_left.at[k], nl_sem + k)
        arrived(from_right.at[k], nr_sem + k)
        value = pair(k, x) + from_left[k].astype(F32) + from_right[k].astype(F32)
        if k < NZ - 1:
            z_out[k] = value.astype(BF16)
            sent_r.append(send(z_out.at[k], z_in.at[k], zr_sem + k, z_peer(k + 1)))
        else:
            total[...] = value

    qz_sem = take(NZ - 1)
    ql_sem, qr_sem, qa_sem, qb_sem = take(), take(), take(), take()
    qs_sem = take()
    base = pl.multiple_of(c * NZ, NZ)
    strip = pl.ds(base, NZ)

    def part_rows(x_, start, size):
        return pl.ds(pl.multiple_of(x_ * QUART + start, BLK), size)

    def spread_1():
        for k in range(1, NDP):
            arrived(extra.at[k - 1, c * NZ + z, quarter], q_sem + k - 1)
        piece = extra.at[:, c * NZ + z, quarter]
        for k in range(1, NZ):
            sent_q.append(send(piece, piece, qz_sem + k - 1, z_peer(k)))

    def spread_2():
        for k in range(1, NZ):
            arrived(extra.at[:, c * NZ + z_at(k), quarter], qz_sem + k - 1)
        piece = extra.at[:, strip, quarter]
        sent_q.append(send(piece, piece, ql_sem, right))
        sent_q.append(send(piece, piece, qr_sem, left))

    def spread_3():
        arrived(extra.at[:, strip, part_rows(xl, 0, QUART)], ql_sem)
        piece = extra.at[:, strip, part_rows(xl, 0, QUART // 2)]
        sent_q.append(send(piece, piece, qa_sem, right))
        arrived(extra.at[:, strip, part_rows(xr, 0, QUART)], qr_sem)
        piece = extra.at[:, strip, part_rows(xr, QUART // 2, QUART // 2)]
        sent_q.append(send(piece, piece, qb_sem, left))

    def spread_4():
        arrived(extra.at[:, strip, part_rows(xo, 0, QUART // 2)], qa_sem)
        arrived(extra.at[:, strip, part_rows(xo, QUART // 2, QUART // 2)], qb_sem)
        piece = extra.at[:, strip]
        sent_q.append(send(piece, piece, qs_sem, sibling))

    stage_a(0)
    stage_a(1)
    stage_b(0)
    spread_1()
    stage_a(2)
    stage_b(1)
    stage_c(0)
    stage_a(3)
    stage_b(2)
    stage_c(1)
    spread_2()
    stage_d(0)
    stage_b(3)
    stage_c(2)
    stage_d(1)
    stage_c(3)
    spread_3()
    stage_d(2)
    stage_d(3)

    value = total[...]
    for k in range(NZ - 1):
        arrived(z_in.at[k], zr_sem + k)
        value = value + z_in[k].astype(F32)
    ret_out[...] = value.astype(BF16)

    yr_sem = take(NY - 1)
    for k in range(1, NY):
        there = pl.ds(pl.multiple_of(wrap(y + k, NY) * BLK, BLK), BLK)
        sent_r.append(send(ret_out.at[there], ret.at[my_rows], yr_sem + k - 1, y_peer(k)))
    ret[my_rows, :] = ret_out[my_rows, :]
    spread_4()

    for k in range(1, NDP):
        arrived(compact.at[k - 1], m_sem + k - 1)
    sides = []
    for k in range(NDP):
        both = compact[k].astype(F32).reshape(NY, BLK // 2, LANES)
        top = jnp.concatenate([both[:, :, : 2 * HID], zeros], axis=2)
        bottom = jnp.concatenate([zeros, both[:, :, 2 * HID :]], axis=2)
        side = jnp.concatenate([top, bottom], axis=1).reshape(ROWS, LANES)
        sides.append(jnp.transpose(side)[: 3 * HID].astype(BF16))
    gbuf[...] = jnp.zeros_like(gbuf)
    other_strip = pl.ds(pl.multiple_of(other * NZ, NZ), NZ)

    def gradient(c_, z_, offset):
        value = jnp.dot(sides[NDP - 1], chunk[at(c_, dp, z_)], preferred_element_type=F32)
        for k in range(1, NDP):
            value += jnp.dot(
                sides[k - 1], extra[k - 1, c_ * NZ + z_], preferred_element_type=F32
            )
        start = offset // 128 * 128
        shift = offset - start
        width = min(LANES + 128, gbuf.shape[1] - start)
        wide = value
        if width > LANES:
            wide = jnp.concatenate([value, jnp.zeros((3 * HID, width - LANES), F32)], axis=1)
        if shift:
            wide = pltpu.roll(wide, shift, 1)
        gbuf[:, start : start + width] += wide

    arrived(extra.at[:, other_strip], qs_sem)
    for z_ in range(NZ):
        for c_ in range(NC):
            gradient(c_, z_, cols * (z_ * NC + c_))
    ggrad[...] = gbuf[:HID].astype(BF16)
    ugrad[...] = gbuf[HID : 2 * HID].astype(BF16)
    dgrad[...] = gbuf[2 * HID :].astype(BF16)

    gates_hi = jnp.where(first_lane, pick * weight_of, 0.0)
    high = gates_hi.astype(BF16)
    low_part = (gates_hi - high.astype(F32)).astype(BF16)
    pick_ret = jnp.where(first_lane, 0.0, pick).astype(BF16)
    for k in range(1, NY):
        from_y = pl.ds(pl.multiple_of(wrap(y + NY - k, NY) * BLK, BLK), BLK)
        arrived(ret.at[from_y], yr_sem + k - 1)
    got = ret[...]
    out = jnp.dot(high, got, preferred_element_type=F32)
    out += jnp.dot(low_part, got, preferred_element_type=F32)
    mixed[...] = out[:, :cols].astype(BF16)
    tgrad[...] = jnp.dot(pick_ret, got, preferred_element_type=F32)[:, :cols].astype(BF16)

    for copy in sent_y + sent_g + sent_q + sent_m + sent_r:
        copy.wait_send()


def per_device(tokens, cotangent, route_ids, gates, w_gate, w_up, w_down):
    rows, cols = tokens.shape
    hid, width = w_gate.shape
    share = width // NDP
    vmem = pl.BlockSpec(memory_space=pltpu.VMEM)
    hbm = pl.BlockSpec(memory_space=pl.ANY)
    chunk_of = (ROWS, LANES)
    return pl.pallas_call(
        kernel,
        out_shape=(
            jax.ShapeDtypeStruct((rows, cols), BF16),
            jax.ShapeDtypeStruct((rows, cols), BF16),
            jax.ShapeDtypeStruct((hid, share), BF16),
            jax.ShapeDtypeStruct((hid, share), BF16),
            jax.ShapeDtypeStruct((hid, share), BF16),
        ),
        in_specs=[vmem] * 4 + [hbm] * 3,
        out_specs=[vmem] * 5,
        scratch_shapes=[
            pltpu.VMEM((3, hid, width), BF16),
            pltpu.VMEM((CHUNKS, LANES, LANES), BF16),
            pltpu.VMEM(chunk_of, BF16),
            pltpu.VMEM((CHUNKS,) + chunk_of, BF16),
            pltpu.VMEM(chunk_of, F32),
            pltpu.VMEM(chunk_of, BF16),
            pltpu.VMEM((NDP, ROWS // 2, LANES), BF16),
            pltpu.VMEM((NDP - 1, NC * NZ) + chunk_of, BF16),
            pltpu.VMEM((NZ, NX) + chunk_of, BF16),
            pltpu.VMEM((NZ, NX) + chunk_of, F32),
            pltpu.VMEM((NZ, NX) + chunk_of, BF16),
            pltpu.VMEM((NZ,) + chunk_of, BF16),
            pltpu.VMEM((NZ, HALF, LANES), BF16),
            pltpu.VMEM((NZ, HALF, LANES), BF16),
            pltpu.VMEM((NZ,) + chunk_of, BF16),
            pltpu.VMEM((NZ,) + chunk_of, BF16),
            pltpu.VMEM((NZ,) + chunk_of, BF16),
            pltpu.VMEM((NZ,) + chunk_of, BF16),
            pltpu.VMEM((NZ - 1,) + chunk_of, BF16),
            pltpu.VMEM((NZ - 1,) + chunk_of, BF16),
            pltpu.VMEM(chunk_of, F32),
            pltpu.VMEM(chunk_of, BF16),
            pltpu.VMEM(chunk_of, BF16),
            pltpu.VMEM((3 * hid, share), F32),
            pltpu.SemaphoreType.DMA((N_SEMS,)),
        ],
        compiler_params=pltpu.CompilerParams(
            collective_id=0, has_side_effects=True, vmem_limit_bytes=44 * 1024 * 1024
        ),
        name="experts",
    )(tokens, cotangent, route_ids, gates, w_gate, w_up, w_down)


def solution(mesh):
    in_specs = (
        P(("dp", "expert"), "tensor"),
        P(("dp", "expert"), "tensor"),
        P(("dp", "expert"), None),
        P(("dp", "expert"), None),
        P(("expert", "tensor"), None),
        P(("expert", "tensor"), None),
        P(("expert", "tensor"), None),
    )
    out_specs = (
        P(("dp", "expert"), "tensor"),
        P(("dp", "expert"), "tensor"),
        P(("expert", "tensor"), "dp"),
        P(("expert", "tensor"), "dp"),
        P(("expert", "tensor"), "dp"),
    )
    return jax.shard_map(
        per_device, mesh=mesh, in_specs=in_specs, out_specs=out_specs, check_vma=False
    )
```

time: 480 us -> 87.8 us (0.18)
  blocking collectives: 193 us -> 0 us
  waiting for transfers between devices: 178 us -> 0 us
  Pallas kernels: 0 us -> 77.3 us
  starting transfers between devices: 43.2 us -> 0 us
  local copies, waits for them, and re-layouts: 33.7 us -> 9.44 us
  matrix products: 15.3 us -> 0 us
  between operations: 14 us -> 0.69 us
    all_gather x1 -> x0, blocking collectives: 193 us -> none  [per_device(): gathered = lax.all_gather(got_rows, 'tensor', axis=2, tiled=True)]
    reduce_scatter x3 -> x0, waiting for transfers between devices: 93.8 us -> none  [the longest x1 57.5 us: per_device(): lax.psum_scatter(down_term.astype(jnp.bfloat16), 'dp', scatter_dimension=...]
    all_to_all x7 -> x0, waiting for transfers between devices: 83.8 us -> none  [the longest x1 44.3 us: per_device(): lax.all_to_all(to_pieces(input_part), 'tensor', split_axis=1, concat_axis...]
    pallas_call x0 -> x1, Pallas kernels: none -> 77.3 us  [per_device(): pl.pallas_call(kernel, out_shape=(jax.ShapeDtypeStruct((rows, cols), BF16...]
    all_to_all x7 -> x0, starting transfers between devices: 42.9 us -> none  [the longest x1 15.6 us: per_device(): lax.all_to_all(wide.reshape(rows_all, n_tensor, part_cols), 'tensor', spl...]
    all_gather x1 -> x0, local copies, waits for them, and re-layouts: 15.4 us -> none  [per_device(): gathered = lax.all_gather(got_rows, 'tensor', axis=2, tiled=True)]
    dot_general x14 -> x0, matrix products: 15.3 us -> none  [the longest x1 2.09 us: per_device(): lax.dot_general(hidden, cot_full, contract_rows, preferred_element_type=j...]
    reshape x6 -> x0, local copies, waits for them, and re-layouts: 11.3 us -> none  [the longest x4 7.82 us: to_pieces(): return full.reshape(rows_all, n_tensor, part_cols)]
  transfers between devices with their start and end apart: 10 -> 0, of which waited for: 8 -> 0; matrix products, arithmetic and copies ran while one was open for 8% -> 0% of each run, Pallas kernels for 0% -> 0%
where the time goes in v1:
time: 87.8 us; the launch traced here: 87.5 us
  Pallas kernels  77.3 us (88%)
  local copies, waits for them, and re-layouts  9.44 us (11%)
    pallas_call x1, Pallas kernels, per_device(): pl.pallas_call(kernel, out_shape=(jax.ShapeDtypeStruct((rows, cols), BF16...  77.3 us
    unnamed x19, local copies, waits for them, and re-layouts  7.99 us

profile of v1, /device:TPU:1, one launch (start us, length us, event | category | flops | bytes accessed | tf_op | source)
XLA Modules:
  0.0 87.5 jit_solution(14400987269856641592)
XLA Ops:
  0.6 0.0 copy-start.3
  0.6 0.9 %copy.12.tok = bf16[128,224]{1,0:T(8,128)(2,1)S(1)} copy(bf16[128,224]{0,1:T(8,128)(2,1)} %param.7) | data formatting | bytes 114688 | tf_op args[0]
  1.6 0.0 copy-done.3
  1.6 0.0 copy-start.4
  1.6 0.1 copy.13.cot
  1.7 0.6 copy-done.4
  2.3 0.0 copy-start.5
  2.3 0.1 copy.14.rid
  2.4 0.6 copy-done.5
  3.0 0.1 copy.15.gat
  3.1 0.0 copy-start
  3.1 1.2 %copy-done = bf16[64,7168]{1,0:T(8,128)(2,1)S(1)} copy-done((bf16[64,7168]{1,0:T(8,128)(2,1)S(1)}, bf16[64,7168]{1,0:T(8,128)(2,1)}, u32[]{:S(2)}) %copy-start) | copy-done | bytes 917528
  4.2 0.0 copy-start.1
  4.3 1.2 %copy-done.1 = bf16[64,7168]{1,0:T(8,128)(2,1)S(1)} copy-done((bf16[64,7168]{1,0:T(8,128)(2,1)S(1)}, bf16[64,7168]{1,0:T(8,128)(2,1)}, u32[]{:S(2)}) %copy-start.1) | copy-done | bytes 917528
  5.4 0.0 copy-start.2
  5.4 1.2 %copy-done.2 = bf16[64,7168]{1,0:T(8,128)(2,1)S(1)} copy-done((bf16[64,7168]{1,0:T(8,128)(2,1)S(1)}, bf16[64,7168]{1,0:T(8,128)(2,1)}, u32[]{:S(2)}) %copy-start.2) | copy-done | bytes 917528
  6.6 77.3 %experts.1 = (bf16[128,224]{1,0:T(8,128)(2,1)S(1)}, bf16[128,224]{1,0:T(8,128)(2,1)S(1)}, bf16[64,1792]{1,0:T(8,128)(2,1)S(1)}, bf16[64,1792]{1,0:T(8,128)(2,1)S(1)}, bf16[64,1792]{1,0:T(8,128)(2,1)S(1)}) custom-call(bf16[128,224]{1,0:T(8,128)(2,1)S(1)} %copy.12.tok, bf16[128,224]{1,0:T(8,128)(2,1)S(1)} %copy.13.cot, s32[128,8]{1,0:T(8,128)S(1)} %copy.14.rid, ...), custom_call_target="tpu_custom_call" | custom-call | tf_op jit(solution)/shard_map/experts/pallas_call | solution.py:425
  84.0 0.7 copy.16
  84.7 0.7 copy.17
  85.4 0.7 copy.21
  86.1 0.7 copy.22
  86.8 0.7 copy.23
Async XLA Ops:
  0.6 1.0 %copy-start.3 = (bf16[128,224]{0,1:T(8,128)(2,1)S(1)}, bf16[128,224]{0,1:T(8,128)(2,1)}, u32[]{:S(2)}) copy-start(bf16[128,224]{0,1:T(8,128)(2,1)} %param.8) | copy-start | bytes 172036
  1.6 0.7 copy-start.4
  2.3 0.7 copy-start.5
  3.1 1.2 %copy-start = (bf16[64,7168]{1,0:T(8,128)(2,1)S(1)}, bf16[64,7168]{1,0:T(8,128)(2,1)}, u32[]{:S(2)}) copy-start(bf16[64,7168]{1,0:T(8,128)(2,1)} %wg.1) | copy-start | bytes 2752516
  4.2 1.2 %copy-start.1 = (bf16[64,7168]{1,0:T(8,128)(2,1)S(1)}, bf16[64,7168]{1,0:T(8,128)(2,1)}, u32[]{:S(2)}) copy-start(bf16[64,7168]{1,0:T(8,128)(2,1)} %wu.1) | copy-start | bytes 2752516
  5.4 1.2 %copy-start.2 = (bf16[64,7168]{1,0:T(8,128)(2,1)S(1)}, bf16[64,7168]{1,0:T(8,128)(2,1)}, u32[]{:S(2)}) copy-start(bf16[64,7168]{1,0:T(8,128)(2,1)} %wd.1) | copy-start | bytes 2752516

commit v2 on v1

v2 whole, which is shorter than its diff:
```python
import jax
import jax.numpy as jnp
from jax import lax
from jax.experimental import pallas as pl
from jax.experimental.pallas import tpu as pltpu
from jax.sharding import PartitionSpec as P

NX, NZ, NC = 4, 4, 2
NY = 8
NDP = 4
CHUNKS = NX * NZ * NC
BLK = 16
ROWS = NY * BLK
REAL = NY * 14
HALF = 64
QUART = ROWS // 4
LANES = 256
HID = 64
N_SEMS = 208
BF16 = jnp.bfloat16
F32 = jnp.float32


def wrap(value, size):
    return lax.rem(value, size)


def nt_dot(left, right):
    return lax.dot_general(left, right, (((1,), (1,)), ((), ())), preferred_element_type=F32)


def tn_dot(left, right):
    return lax.dot_general(left, right, (((0,), (0,)), ((), ())), preferred_element_type=F32)


def kernel(
    tok_in, cot_in, rid_in, gat_in, wg, wu, wd,
    mixed, tgrad, ggrad, ugrad, dgrad,
    tok, cot, rid, gat, wraw, wt, disp, landed, chunk, acc, mine, compact,
    extra, part, kept, sib_in, opp_out, opp_a, opp_b, opp_in, right_out, left_out,
    from_left, from_right, z_out, z_in, total, ret_out, ret, gpart, gbuf, sems, ready,
):
    dp = lax.axis_index("dp")
    y = lax.axis_index("expert")
    t = lax.axis_index("tensor")
    x = t // (NZ * NC)
    z = wrap(t // NC, NZ)
    c = wrap(t, NC)
    other = 1 - c
    xr, xl, xo = wrap(x + 1, NX), wrap(x + 3, NX), wrap(x + 2, NX)
    cols = tok.shape[0]
    count = [0]

    def take(n=1):
        base = count[0]
        count[0] += n
        assert count[0] <= N_SEMS
        return base

    def tensor_at(x_, z_, c_):
        return {"tensor": x_ * (NZ * NC) + z_ * NC + c_}

    def at(c_, x_, z_):
        return c_ * (NX * NZ) + x_ * NZ + z_

    sibling = tensor_at(x, z, other)
    right, left = tensor_at(xr, z, c), tensor_at(xl, z, c)

    def z_peer(k):
        return tensor_at(x, wrap(z + k, NZ), c)

    def y_peer(k):
        return {"expert": wrap(y + k, NY)}

    def dp_peer(k):
        return {"dp": wrap(dp + k, NDP)}

    barrier = pltpu.get_barrier_semaphore()
    partners = [y_peer(k) for k in range(1, NY)]
    partners += [z_peer(k) for k in range(1, NZ)]
    partners += [dp_peer(1), dp_peer(NDP - 1)]
    partners += [sibling, right, left, tensor_at(xo, z, c)]
    for where in partners:
        pl.semaphore_signal(barrier, inc=1, device_id=where, device_id_type=pl.DeviceIdType.MESH)

    def send(src, dst, recv, where):
        copy = pltpu.make_async_remote_copy(
            src_ref=src, dst_ref=dst, send_sem=sems.at[take()], recv_sem=sems.at[recv],
            device_id=where, device_id_type=pl.DeviceIdType.MESH,
        )
        copy.start()
        return copy

    def arrived(ref, sem):
        pltpu.make_async_copy(ref, ref, sems.at[sem]).wait()

    small = []
    for src, dst in ((rid_in, rid), (gat_in, gat), (tok_in, tok), (cot_in, cot)):
        small.append(pltpu.make_async_copy(src, dst, sems.at[take()]))
        small[-1].start()
    loads = []
    for i, ref in enumerate((wg, wu, wd)):
        loads.append(pltpu.make_async_copy(ref, wraw.at[i], sems.at[take()]))
        loads[-1].start()

    lane = lax.broadcasted_iota(jnp.int32, (ROWS, ROWS), 1)
    row = lax.broadcasted_iota(jnp.int32, (ROWS, ROWS), 0)
    label = row // BLK
    first = wrap(row // (BLK // 2), 2) == 0
    slot = wrap(row, BLK // 2)
    upto = jnp.where(row <= lane, 1.0, 0.0).astype(BF16)

    def packed(at_):
        place = wrap(at_, BLK // 2)
        half = wrap(at_ // (BLK // 2), 2)
        return jnp.where(place < 7, (REAL // 2) * half + 7 * (at_ // BLK) + place, -1)

    pack = jnp.where(row == packed(lane), 1.0, 0.0).astype(BF16)
    unpack = jnp.where(lane == packed(row), 1.0, 0.0).astype(BF16)
    disp[...] = jnp.zeros_like(disp)
    small[0].wait()
    small[1].wait()
    hits = jnp.zeros((ROWS, ROWS), F32)
    weight_of = jnp.zeros((ROWS, ROWS), F32)
    for k in range(rid.shape[0]):
        same = rid[k : k + 1, :] == label
        hits = hits + jnp.where(same, 1.0, 0.0)
        weight_of = weight_of + jnp.where(same, gat[k : k + 1, :], 0.0)
    places = jnp.dot(hits.astype(BF16), upto, preferred_element_type=F32) - 1.0
    pick = jnp.where((hits == 1.0) & (places == slot.astype(F32)), 1.0, 0.0)
    slot_gate = jnp.sum(pick * weight_of, axis=1, keepdims=True)
    pick_tok = jnp.where(first, pick, 0.0).astype(BF16)
    pick_cot = jnp.where(first, 0.0, pick).astype(BF16)
    small[2].wait()
    small[3].wait()
    rows_tok = nt_dot(pick_tok, tok[...])
    rows_cot = nt_dot(pick_cot, cot[...])
    disp[:, 0:cols] = (rows_tok + slot_gate * rows_cot).astype(BF16)

    pl.semaphore_wait(barrier, len(partners))
    pl.semaphore_signal(
        ready, inc=1, device_id=dp_peer(NDP - 1), device_id_type=pl.DeviceIdType.MESH
    )

    me = at(c, x, z)
    my_rows = pl.ds(pl.multiple_of(y * BLK, BLK), BLK)
    sent_y = []
    y_in = take(NY - 1)
    for k in range(1, NY):
        there = pl.ds(pl.multiple_of(wrap(y + k, NY) * BLK, BLK), BLK)
        sent_y.append(send(disp.at[there], landed.at[my_rows], y_in + k - 1, y_peer(k)))
    landed[my_rows, :] = disp[my_rows, :]
    chunk[:, REAL:, :] = jnp.zeros((CHUNKS, ROWS - REAL, LANES), BF16)

    for copy in loads:
        copy.wait()
    wt[:, :, LANES // 2 :] = jnp.zeros((CHUNKS, LANES, LANES // 2), BF16)
    wt[:, 3 * HID :, : LANES // 2] = jnp.zeros((CHUNKS, LANES - 3 * HID, LANES // 2), BF16)
    for tt in range(CHUNKS):
        g = at(tt % NC, tt // (NZ * NC), (tt // NC) % NZ)
        for i in range(3):
            wt[g, HID * i : HID * (i + 1), 0:cols] = wraw[i, :, cols * tt : cols * (tt + 1)]
    acc[...] = jnp.zeros_like(acc)

    for k in range(1, NY):
        from_y = pl.ds(pl.multiple_of(wrap(y + NY - k, NY) * BLK, BLK), BLK)
        arrived(landed.at[from_y], y_in + k - 1)
    chunk[me] = jnp.dot(pack, landed[...], preferred_element_type=F32).astype(BF16)

    def consume(g):
        acc[...] += nt_dot(chunk[g], wt[g])

    sib_sem = take(NX * NZ)
    z_sem = take(NZ - 1)
    left_sem, right_sem = take(NZ), take(NZ)
    oa_sem, ob_sem = take(NZ), take(NZ)
    sent_g = []
    sent_q = []
    opposite = tensor_at(xo, z, c)
    straight = (0, NZ - 1)

    def real(g, start=0, size=REAL):
        return chunk.at[g, pl.ds(start, size)]

    def pass_on(ref, sem, where):
        sent_g.append(send(ref, ref, sem, where))

    def to_sibling(x_, k):
        zk = z_at(k)
        pass_on(real(at(c, x_, zk)), sib_sem + x_ * NZ + zk, sibling)
        consume(at(c, x_, zk))

    def sibling_has(x_, k):
        zk = z_at(k)
        g = at(other, x_, zk)
        arrived(real(g), sib_sem + x_ * NZ + zk)
        consume(g)

    def z_at(k):
        return wrap(z + NZ - k, NZ)

    def from_z(k):
        zk = z_at(k)
        g = at(c, x, zk)
        if k > 0:
            arrived(real(g), z_sem + k - 1)
        pass_on(real(g), left_sem + zk, right)
        pass_on(real(g), right_sem + zk, left)
        if k in straight:
            pass_on(real(g), oa_sem + zk, opposite)
        if k == 0:
            for j in range(1, NZ):
                pass_on(real(g), z_sem + j - 1, z_peer(j))
        to_sibling(x, k)

    def from_x(k):
        zk = z_at(k)
        g = at(c, xl, zk)
        arrived(real(g), left_sem + zk)
        if k not in straight:
            pass_on(real(g, 0, HALF), oa_sem + zk, right)
        to_sibling(xl, k)
        g = at(c, xr, zk)
        arrived(real(g), right_sem + zk)
        if k not in straight:
            pass_on(real(g, HALF, REAL - HALF), ob_sem + zk, left)
        to_sibling(xr, k)

    def from_o(k):
        zk = z_at(k)
        g = at(c, xo, zk)
        if k in straight:
            arrived(real(g), oa_sem + zk)
        else:
            arrived(real(g, 0, HALF), oa_sem + zk)
            arrived(real(g, HALF, REAL - HALF), ob_sem + zk)
        to_sibling(xo, k)

    quarter = pl.ds(pl.multiple_of(x * QUART, QUART), QUART)
    q_sem = take(NDP - 1)

    def across():
        pl.semaphore_wait(ready, 1)
        for k in range(1, NDP):
            src = chunk.at[at(c, wrap(dp + k, NDP), z), quarter]
            sent_q.append(send(src, extra.at[k - 1, c * NZ + z, quarter], q_sem + k - 1, dp_peer(k)))

    from_z(0)
    from_z(1)
    from_x(0)
    sibling_has(x, 0)
    from_z(2)
    from_o(0)
    across()
    from_x(1)
    sibling_has(x, 1)
    from_z(3)
    sibling_has(xl, 0)
    sibling_has(xr, 0)
    from_x(2)
    sibling_has(x, 2)
    sibling_has(xo, 0)
    from_o(1)
    sibling_has(xl, 1)
    sibling_has(xr, 1)
    sibling_has(x, 3)
    from_x(3)
    sibling_has(xl, 2)
    sibling_has(xr, 2)
    from_o(2)
    sibling_has(xo, 1)
    from_o(3)
    sibling_has(xl, 3)
    sibling_has(xr, 3)
    sibling_has(xo, 2)
    sibling_has(xo, 3)

    half_rows = REAL // 2
    fwd = acc[:half_rows, : 2 * HID]
    bwd = acc[half_rows:REAL, 2 * HID :]
    low = lax.broadcasted_iota(jnp.int32, (half_rows, 2 * HID), 1) < HID
    turned = pltpu.roll(fwd, HID, 1)
    pre = jnp.where(low, fwd, turned)
    upper = jnp.where(low, turned, fwd)
    back = bwd + pltpu.roll(bwd, HID, 1)
    sig = jax.nn.sigmoid(pre)
    act = pre * sig
    hidden = act * upper
    gate_delta = back * upper * sig * (1.0 + pre * (1.0 - sig))
    up_delta = back * act
    deltas = jnp.where(low, gate_delta, up_delta)
    hid = jnp.where(low, hidden, 0.0)
    zeros = jnp.zeros((half_rows, 2 * HID), F32)
    pad = jnp.zeros((ROWS // 2 - half_rows, LANES), F32)
    tail = jnp.zeros((ROWS - REAL, LANES), F32)
    compact[NDP - 1] = jnp.concatenate(
        [jnp.concatenate([deltas, hid], axis=1), pad], axis=0
    ).astype(BF16)
    top = jnp.concatenate([zeros, hid], axis=1)
    bottom = jnp.concatenate([deltas, zeros], axis=1)
    mine[...] = jnp.concatenate([top, bottom, tail], axis=0).astype(BF16)

    m_sem = take(NDP - 1)
    sent_m = []
    for k in range(1, NDP):
        sent_m.append(send(compact.at[NDP - 1], compact.at[k - 1], m_sem + k - 1, dp_peer(k)))

    sr_sem = take(NZ)
    xa_sem, xb_sem = take(NZ), take(NZ)
    nl_sem, nr_sem = take(NZ), take(NZ)
    zr_sem = take(NZ - 1)
    sent_r = []

    def stage_a(k):
        zk = wrap(z + k + 1, NZ)
        left_side = mine[...]

        def one(x_, carry):
            part[k, x_] = jnp.dot(
                left_side, wt[at(other, x_, zk)], preferred_element_type=F32
            ).astype(BF16)
            return carry

        lax.fori_loop(0, NX, one, 0)
        rows = pl.ds(0, REAL)
        sent_r.append(send(part.at[k, :, rows], sib_in.at[k, :, rows], sr_sem + k, sibling))

        def two(x_, carry):
            kept[k, x_] = jnp.dot(left_side, wt[at(c, x_, zk)], preferred_element_type=F32)
            return carry

        lax.fori_loop(0, NX, two, 0)

    def pair(k, x_):
        return kept[k, x_, :REAL] + sib_in[k, x_, :REAL].astype(F32)

    def stage_b(k):
        arrived(sib_in.at[k, :, pl.ds(0, REAL)], sr_sem + k)
        opp_out[k] = pair(k, xo).astype(BF16)
        if k in straight:
            sent_r.append(send(opp_out.at[k], opp_in.at[k // (NZ - 1)], xa_sem + k, opposite))
            return
        sent_r.append(send(opp_out.at[k, pl.ds(0, HALF)], opp_a.at[k], xa_sem + k, right))
        sent_r.append(send(opp_out.at[k, pl.ds(HALF, REAL - HALF)], opp_b.at[k], xb_sem + k, left))

    def stage_c(k):
        value = pair(k, xr)
        if k in straight:
            right_out[k] = value.astype(BF16)
        else:
            arrived(opp_a.at[k], xa_sem + k)
            right_out[k, :HALF] = (value[:HALF] + opp_a[k].astype(F32)).astype(BF16)
            right_out[k, HALF:] = value[HALF:].astype(BF16)
        sent_r.append(send(right_out.at[k], from_left.at[k], nl_sem + k, right))
        value = pair(k, xl)
        if k in straight:
            left_out[k] = value.astype(BF16)
        else:
            arrived(opp_b.at[k], xb_sem + k)
            left_out[k, :HALF] = value[:HALF].astype(BF16)
            left_out[k, HALF:] = (value[HALF:] + opp_b[k].astype(F32)).astype(BF16)
        sent_r.append(send(left_out.at[k], from_right.at[k], nr_sem + k, left))

    def stage_d(k):
        arrived(from_left.at[k], nl_sem + k)
        arrived(from_right.at[k], nr_sem + k)
        value = pair(k, x) + from_left[k].astype(F32) + from_right[k].astype(F32)
        if k in straight:
            arrived(opp_in.at[k // (NZ - 1)], xa_sem + k)
            value = value + opp_in[k // (NZ - 1)].astype(F32)
        if k < NZ - 1:
            z_out[k] = value.astype(BF16)
            sent_r.append(send(z_out.at[k], z_in.at[k], zr_sem + k, z_peer(k + 1)))
        else:
            total[...] = value

    qz_sem = take(NZ - 1)
    ql_sem, qr_sem, qa_sem, qb_sem = take(NZ), take(NZ), take(NZ), take(NZ)
    qs_sem = take(NZ)

    def part_rows(x_, start, size):
        return pl.ds(pl.multiple_of(x_ * QUART + start, BLK), size)

    def spread_1():
        for k in range(1, NDP):
            arrived(extra.at[k - 1, c * NZ + z, quarter], q_sem + k - 1)
        piece = extra.at[:, c * NZ + z, quarter]
        for k in range(1, NZ):
            sent_q.append(send(piece, piece, qz_sem + k - 1, z_peer(k)))
        sent_q.append(send(piece, piece, ql_sem + 0, right))
        sent_q.append(send(piece, piece, qr_sem + 0, left))

    def spread_2(k):
        piece = extra.at[:, c * NZ + z_at(k), quarter]
        arrived(piece, qz_sem + k - 1)
        sent_q.append(send(piece, piece, ql_sem + k, right))
        sent_q.append(send(piece, piece, qr_sem + k, left))

    def spread_3(k):
        here = c * NZ + z_at(k)
        arrived(extra.at[:, here, part_rows(xl, 0, QUART)], ql_sem + k)
        piece = extra.at[:, here, part_rows(xl, 0, QUART // 2)]
        sent_q.append(send(piece, piece, qa_sem + k, right))
        arrived(extra.at[:, here, part_rows(xr, 0, QUART)], qr_sem + k)
        piece = extra.at[:, here, part_rows(xr, QUART // 2, QUART // 2)]
        sent_q.append(send(piece, piece, qb_sem + k, left))

    def spread_4(k):
        here = c * NZ + z_at(k)
        arrived(extra.at[:, here, part_rows(xo, 0, QUART // 2)], qa_sem + k)
        arrived(extra.at[:, here, part_rows(xo, QUART // 2, QUART // 2)], qb_sem + k)
        piece = extra.at[:, here]
        sent_q.append(send(piece, piece, qs_sem + k, sibling))

    stage_a(0)
    stage_a(1)
    stage_b(0)
    stage_c(0)
    stage_a(2)
    stage_b(1)
    spread_1()
    stage_a(3)
    stage_b(2)
    stage_c(1)
    stage_d(0)
    stage_c(2)
    stage_d(1)
    spread_2(1)
    stage_b(3)
    stage_c(3)
    spread_3(0)
    spread_2(2)
    spread_2(3)
    stage_d(2)
    stage_d(3)

    value = total[...]
    for k in range(NZ - 1):
        arrived(z_in.at[k], zr_sem + k)
        value = value + z_in[k].astype(F32)
    ret_out[...] = jnp.dot(
        unpack[:, :REAL], value.astype(BF16), preferred_element_type=F32
    ).astype(BF16)

    yr_sem = take(NY - 1)
    for k in range(1, NY):
        there = pl.ds(pl.multiple_of(wrap(y + k, NY) * BLK, BLK), BLK)
        sent_r.append(send(ret_out.at[there], ret.at[my_rows], yr_sem + k - 1, y_peer(k)))
    ret[my_rows, :] = ret_out[my_rows, :]
    spread_4(0)
    for k in range(1, NZ):
        spread_3(k)
    for k in range(1, NZ):
        spread_4(k)

    for k in range(1, NDP):
        arrived(compact.at[k - 1], m_sem + k - 1)
    sides = []
    for k in range(NDP):
        both = compact[k, :half_rows].astype(F32)
        top = jnp.concatenate([both[:, : 2 * HID], zeros], axis=1)
        bottom = jnp.concatenate([zeros, both[:, 2 * HID :]], axis=1)
        side = jnp.concatenate([top, bottom, tail], axis=0)
        sides.append(jnp.transpose(side)[: 3 * HID].astype(BF16))
    def gradient(k):
        z_ = z_at(k)
        arrived(extra.at[:, other * NZ + z_], qs_sem + k)
        for c_ in range(NC):
            value = jnp.dot(sides[NDP - 1], chunk[at(c_, dp, z_)], preferred_element_type=F32)
            for j in range(1, NDP):
                value += jnp.dot(
                    sides[j - 1], extra[j - 1, c_ * NZ + z_], preferred_element_type=F32
                )
            gpart[z_ * NC + c_] = value

    for copy in sent_y + sent_g:
        copy.wait_send()
    gradient(0)
    gradient(1)
    gradient(2)

    gate_of = jnp.where(first, pick * weight_of, 0.0)
    high = gate_of.astype(BF16)
    low_part = (gate_of - high.astype(F32)).astype(BF16)
    for k in range(1, NY):
        from_y = pl.ds(pl.multiple_of(wrap(y + NY - k, NY) * BLK, BLK), BLK)
        arrived(ret.at[from_y], yr_sem + k - 1)
    got = ret[...]
    out = tn_dot(got, high) + tn_dot(got, low_part)
    mixed[...] = out[:cols].astype(BF16)
    tgrad[...] = tn_dot(got, pick_cot)[:cols].astype(BF16)

    gradient(3)
    gbuf[...] = jnp.zeros_like(gbuf)
    for i in range(NZ * NC):
        start = cols * i // 128 * 128
        shift = cols * i - start
        width = min(LANES + 128, gbuf.shape[1] - start)
        wide = gpart[i]
        if width > LANES:
            wide = jnp.concatenate([wide, jnp.zeros((3 * HID, width - LANES), F32)], axis=1)
        if shift:
            wide = pltpu.roll(wide, shift, 1)
        gbuf[:, start : start + width] += wide
    ggrad[...] = gbuf[:HID].astype(BF16)
    ugrad[...] = gbuf[HID : 2 * HID].astype(BF16)
    dgrad[...] = gbuf[2 * HID :].astype(BF16)

    for copy in sent_q + sent_m + sent_r:
        copy.wait_send()


def write_out(*refs):
    count = len(refs) // 2
    sems = refs[-1]
    copies = [
        pltpu.make_async_copy(refs[i], refs[count + i], sems.at[i]) for i in range(count)
    ]
    for copy in copies:
        copy.start()
    for copy in copies:
        copy.wait()


def per_device(tokens, cotangent, route_ids, gates, w_gate, w_up, w_down):
    rows, cols = tokens.shape
    hid, width = w_gate.shape
    share = width // NDP
    top = route_ids.shape[1]
    vmem = pl.BlockSpec(memory_space=pltpu.VMEM)
    hbm = pl.BlockSpec(memory_space=pl.ANY)
    chunk_of = (ROWS, LANES)
    real_of = (REAL, LANES)
    shapes = (
        jax.ShapeDtypeStruct((cols, rows), BF16),
        jax.ShapeDtypeStruct((cols, rows), BF16),
        jax.ShapeDtypeStruct((hid, share), BF16),
        jax.ShapeDtypeStruct((hid, share), BF16),
        jax.ShapeDtypeStruct((hid, share), BF16),
    )
    operands = (tokens.T, cotangent.T, route_ids.T, gates.T, w_gate, w_up, w_down)
    results = pl.pallas_call(
        kernel,
        out_shape=shapes,
        in_specs=[hbm] * 7,
        out_specs=[vmem] * 5,
        scratch_shapes=[
            pltpu.VMEM((cols, rows), BF16),
            pltpu.VMEM((cols, rows), BF16),
            pltpu.VMEM((top, rows), jnp.int32),
            pltpu.VMEM((top, rows), F32),
            pltpu.VMEM((3, hid, width), BF16),
            pltpu.VMEM((CHUNKS, LANES, LANES), BF16),
            pltpu.VMEM(chunk_of, BF16),
            pltpu.VMEM(chunk_of, BF16),
            pltpu.VMEM((CHUNKS,) + chunk_of, BF16),
            pltpu.VMEM(chunk_of, F32),
            pltpu.VMEM(chunk_of, BF16),
            pltpu.VMEM((NDP, ROWS // 2, LANES), BF16),
            pltpu.VMEM((NDP - 1, NC * NZ) + chunk_of, BF16),
            pltpu.VMEM((NZ, NX) + chunk_of, BF16),
            pltpu.VMEM((NZ, NX) + chunk_of, F32),
            pltpu.VMEM((NZ, NX) + chunk_of, BF16),
            pltpu.VMEM((NZ,) + real_of, BF16),
            pltpu.VMEM((NZ, HALF, LANES), BF16),
            pltpu.VMEM((NZ, REAL - HALF, LANES), BF16),
            pltpu.VMEM((2,) + real_of, BF16),
            pltpu.VMEM((NZ,) + real_of, BF16),
            pltpu.VMEM((NZ,) + real_of, BF16),
            pltpu.VMEM((NZ,) + real_of, BF16),
            pltpu.VMEM((NZ,) + real_of, BF16),
            pltpu.VMEM((NZ - 1,) + real_of, BF16),
            pltpu.VMEM((NZ - 1,) + real_of, BF16),
            pltpu.VMEM(real_of, F32),
            pltpu.VMEM(chunk_of, BF16),
            pltpu.VMEM(chunk_of, BF16),
            pltpu.VMEM((NZ * NC, 3 * hid, LANES), F32),
            pltpu.VMEM((3 * hid, share), F32),
            pltpu.SemaphoreType.DMA((N_SEMS,)),
            pltpu.SemaphoreType.REGULAR,
        ],
        compiler_params=pltpu.CompilerParams(
            collective_id=0, has_side_effects=True, vmem_limit_bytes=40 * 1024 * 1024
        ),
        name="experts",
    )(*[pltpu.with_memory_space_constraint(v, pltpu.HBM) for v in operands])
    results = pl.pallas_call(
        write_out,
        out_shape=shapes,
        in_specs=[vmem] * 5,
        out_specs=[hbm] * 5,
        scratch_shapes=[pltpu.SemaphoreType.DMA((5,))],
        compiler_params=pltpu.CompilerParams(vmem_limit_bytes=40 * 1024 * 1024),
        name="write_out",
    )(*results)
    return (results[0].T, results[1].T) + tuple(results[2:])


def solution(mesh):
    in_specs = (
        P(("dp", "expert"), "tensor"),
        P(("dp", "expert"), "tensor"),
        P(("dp", "expert"), None),
        P(("dp", "expert"), None),
        P(("expert", "tensor"), None),
        P(("expert", "tensor"), None),
        P(("expert", "tensor"), None),
    )
    out_specs = (
        P(("dp", "expert"), "tensor"),
        P(("dp", "expert"), "tensor"),
        P(("expert", "tensor"), "dp"),
        P(("expert", "tensor"), "dp"),
        P(("expert", "tensor"), "dp"),
    )
    return jax.shard_map(
        per_device, mesh=mesh, in_specs=in_specs, out_specs=out_specs, check_vma=False
    )
```

time: 87.8 us -> 72.6 us (0.83)
  local copies, waits for them, and re-layouts: 9.44 us -> 0 us
  Pallas kernels: 77.3 us -> 71.8 us
    unnamed x19 -> x0, local copies, waits for them, and re-layouts: 7.99 us -> none
    pallas_call x1 -> x2, Pallas kernels: 77.3 us -> 71.8 us  [the longest x1 70.8 us: per_device(): pl.pallas_call(kernel, out_shape=shapes, in_specs=[hbm] * 7, out_specs=[v...]
    pallas_call x2 -> x0, local copies, waits for them, and re-layouts: 1.45 us -> none  [per_device(): pl.pallas_call(kernel, out_shape=(jax.ShapeDtypeStruct((rows, cols), BF16...]
where the time goes in v2:
time: 72.6 us; the launch traced here: 72.4 us
  Pallas kernels  71.8 us (99%)
    pallas_call x1, Pallas kernels, per_device(): pl.pallas_call(kernel, out_shape=shapes, in_specs=[hbm] * 7, out_specs=[v...  70.8 us

profile of v2, /device:TPU:1, one launch (start us, length us, event | category | flops | bytes accessed | tf_op | source)
XLA Modules:
  0.0 72.4 jit_solution(6072244651992714983)
XLA Ops:
  0.6 70.8 %experts.1 = (bf16[224,128]{1,0:T(8,128)(2,1)S(1)}, bf16[224,128]{1,0:T(8,128)(2,1)S(1)}, bf16[64,1792]{1,0:T(8,128)(2,1)S(1)}, bf16[64,1792]{1,0:T(8,128)(2,1)S(1)}, bf16[64,1792]{1,0:T(8,128)(2,1)S(1)}) custom-call(bf16[224,128]{1,0:T(8,128)(2,1)} %bitcast.6, bf16[224,128]{1,0:T(8,128)(2,1)} %bitcast.7, s32[8,128]{1,0:T(8,128)} %bitcast.8, ...), custom_call_target="tpu_custom_call" | custom-call | tf_op jit(solution)/shard_map/experts/pallas_call | solution.py:542
  71.5 0.9 %write_out.1 = (bf16[224,128]{1,0:T(8,128)(2,1)}, bf16[224,128]{1,0:T(8,128)(2,1)}, bf16[64,1792]{1,0:T(8,128)(2,1)}, bf16[64,1792]{1,0:T(8,128)(2,1)}, bf16[64,1792]{1,0:T(8,128)(2,1)}) custom-call(bf16[224,128]{1,0:T(8,128)(2,1)S(1)} %get-tuple-element.15.refs_0_, bf16[224,128]{1,0:T(8,128)(2,1)S(1)} %get-tuple-element.16.refs_1_, ...), custom_call_target="tpu_custom_call" | custom-call | tf_op jit(solution)/shard_map/write_out/pallas_call | solution.py:587

commit v3 on v2

--- a/solution.py
+++ b/solution.py
@@ -16,7 +16,7 @@
 QUART = ROWS // 4
 LANES = 256
 HID = 64
-N_SEMS = 208
+N_SEMS = 240
 BF16 = jnp.bfloat16
 F32 = jnp.float32
 
@@ -36,8 +36,8 @@
 def kernel(
     tok_in, cot_in, rid_in, gat_in, wg, wu, wd,
     mixed, tgrad, ggrad, ugrad, dgrad,
-    tok, cot, rid, gat, wraw, wt, disp, landed, chunk, acc, mine, compact,
-    extra, part, kept, sib_in, opp_out, opp_a, opp_b, opp_in, right_out, left_out,
+    tok, cot, rid, gat, wraw, wt, disp, landed, chunk, acc, acc_sib, acc_in, mine, theirs, wsib, compact,
+    extra, kept, opp_out, opp_a, opp_b, opp_in, right_out, left_out,
     from_left, from_right, z_out, z_in, total, ret_out, ret, gpart, gbuf, sems, ready,
 ):
     dp = lax.axis_index("dp")
@@ -63,11 +63,16 @@
     def at(c_, x_, z_):
         return c_ * (NX * NZ) + x_ * NZ + z_
 
+    upper_z = z // 2
+
+    def z_at(k):
+        return (z, 1 - z + 4 * upper_z, 2 - upper_z, 3 - 3 * upper_z)[k]
+
     sibling = tensor_at(x, z, other)
     right, left = tensor_at(xr, z, c), tensor_at(xl, z, c)
 
     def z_peer(k):
-        return tensor_at(x, wrap(z + k, NZ), c)
+        return tensor_at(x, z_at(k), c)
 
     def y_peer(k):
         return {"expert": wrap(y + k, NY)}
@@ -161,17 +166,26 @@
         for i in range(3):
             wt[g, HID * i : HID * (i + 1), 0:cols] = wraw[i, :, cols * tt : cols * (tt + 1)]
     acc[...] = jnp.zeros_like(acc)
+    acc_sib[...] = jnp.zeros_like(acc_sib)
+    wsib[:, 3 * HID :, :] = jnp.zeros((NX * NZ, LANES - 3 * HID, LANES), BF16)
+    w_sem = take()
+    held = pl.ds(0, 3 * HID)
+    give = pl.ds(pl.multiple_of(other * (NX * NZ), NX * NZ), NX * NZ)
+    sent_w = [send(wt.at[give, held], wsib.at[:, held], w_sem, sibling)]
 
     for k in range(1, NY):
         from_y = pl.ds(pl.multiple_of(wrap(y + NY - k, NY) * BLK, BLK), BLK)
         arrived(landed.at[from_y], y_in + k - 1)
     chunk[me] = jnp.dot(pack, landed[...], preferred_element_type=F32).astype(BF16)
 
-    def consume(g):
-        acc[...] += nt_dot(chunk[g], wt[g])
-
-    sib_sem = take(NX * NZ)
-    z_sem = take(NZ - 1)
+    def consume(x_, k):
+        zk = z_at(k)
+        g = at(c, x_, zk)
+        value = chunk[g]
+        acc[...] += nt_dot(value, wt[g])
+        acc_sib[...] += nt_dot(value, wsib[x_ * NZ + zk])
+
+    z_sem = take(NZ)
     left_sem, right_sem = take(NZ), take(NZ)
     oa_sem, ob_sem = take(NZ), take(NZ)
     sent_g = []
@@ -185,33 +199,18 @@
     def pass_on(ref, sem, where):
         sent_g.append(send(ref, ref, sem, where))
 
-    def to_sibling(x_, k):
-        zk = z_at(k)
-        pass_on(real(at(c, x_, zk)), sib_sem + x_ * NZ + zk, sibling)
-        consume(at(c, x_, zk))
-
-    def sibling_has(x_, k):
-        zk = z_at(k)
-        g = at(other, x_, zk)
-        arrived(real(g), sib_sem + x_ * NZ + zk)
-        consume(g)
-
-    def z_at(k):
-        return wrap(z + NZ - k, NZ)
-
     def from_z(k):
         zk = z_at(k)
         g = at(c, x, zk)
         if k > 0:
-            arrived(real(g), z_sem + k - 1)
+            arrived(real(g), z_sem + zk)
         pass_on(real(g), left_sem + zk, right)
         pass_on(real(g), right_sem + zk, left)
         if k in straight:
             pass_on(real(g), oa_sem + zk, opposite)
         if k == 0:
             for j in range(1, NZ):
-                pass_on(real(g), z_sem + j - 1, z_peer(j))
-        to_sibling(x, k)
+                pass_on(real(g), z_sem + z, z_peer(j))
 
     def from_x(k):
         zk = z_at(k)
@@ -219,12 +218,10 @@
         arrived(real(g), left_sem + zk)
         if k not in straight:
             pass_on(real(g, 0, HALF), oa_sem + zk, right)
-        to_sibling(xl, k)
         g = at(c, xr, zk)
         arrived(real(g), right_sem + zk)
         if k not in straight:
             pass_on(real(g, HALF, REAL - HALF), ob_sem + zk, left)
-        to_sibling(xr, k)
 
     def from_o(k):
         zk = z_at(k)
@@ -234,7 +231,6 @@
         else:
             arrived(real(g, 0, HALF), oa_sem + zk)
             arrived(real(g, HALF, REAL - HALF), ob_sem + zk)
-        to_sibling(xo, k)
 
     quarter = pl.ds(pl.multiple_of(x * QUART, QUART), QUART)
     q_sem = take(NDP - 1)
@@ -248,32 +244,43 @@
     from_z(0)
     from_z(1)
     from_x(0)
-    sibling_has(x, 0)
     from_z(2)
     from_o(0)
     across()
     from_x(1)
-    sibling_has(x, 1)
+    arrived(wsib.at[:, held], w_sem)
+    consume(x, 0)
+    consume(x, 1)
     from_z(3)
-    sibling_has(xl, 0)
-    sibling_has(xr, 0)
+    consume(xl, 0)
+    consume(xr, 0)
+    consume(x, 2)
     from_x(2)
-    sibling_has(x, 2)
-    sibling_has(xo, 0)
+    consume(xo, 0)
+    consume(xl, 1)
+    consume(xr, 1)
     from_o(1)
-    sibling_has(xl, 1)
-    sibling_has(xr, 1)
-    sibling_has(x, 3)
+    consume(x, 3)
+    consume(xl, 2)
+    consume(xr, 2)
     from_x(3)
-    sibling_has(xl, 2)
-    sibling_has(xr, 2)
+    consume(xo, 1)
     from_o(2)
-    sibling_has(xo, 1)
+    consume(xl, 3)
+    consume(xr, 3)
+    consume(xo, 2)
     from_o(3)
-    sibling_has(xl, 3)
-    sibling_has(xr, 3)
-    sibling_has(xo, 2)
-    sibling_has(xo, 3)
+    consume(xo, 3)
+
+    acc_sem, slots_sem, theirs_sem = take(), take(), take()
+    own_rows = pl.ds(0, REAL)
+    sent_w.append(send(acc_sib.at[own_rows], acc_in, acc_sem, sibling))
+    mine_at = pl.ds(pl.multiple_of(c * (NX * NZ) + dp * NZ, NZ), NZ)
+    other_at = pl.ds(pl.multiple_of(other * (NX * NZ) + dp * NZ, NZ), NZ)
+    slots = chunk.at[mine_at, own_rows]
+    sent_w.append(send(slots, slots, slots_sem, sibling))
+    arrived(acc_in, acc_sem)
+    acc[:REAL] += acc_in[...]
 
     half_rows = REAL // 2
     fwd = acc[:half_rows, : 2 * HID]
@@ -293,49 +300,40 @@
     zeros = jnp.zeros((half_rows, 2 * HID), F32)
     pad = jnp.zeros((ROWS // 2 - half_rows, LANES), F32)
     tail = jnp.zeros((ROWS - REAL, LANES), F32)
+    top = jnp.concatenate([zeros, hid], axis=1)
+    bottom = jnp.concatenate([deltas, zeros], axis=1)
+    mine[...] = jnp.concatenate([top, bottom, tail], axis=0).astype(BF16)
+
+    sent_w.append(send(mine, theirs, theirs_sem, sibling))
     compact[NDP - 1] = jnp.concatenate(
         [jnp.concatenate([deltas, hid], axis=1), pad], axis=0
     ).astype(BF16)
-    top = jnp.concatenate([zeros, hid], axis=1)
-    bottom = jnp.concatenate([deltas, zeros], axis=1)
-    mine[...] = jnp.concatenate([top, bottom, tail], axis=0).astype(BF16)
-
     m_sem = take(NDP - 1)
     sent_m = []
     for k in range(1, NDP):
         sent_m.append(send(compact.at[NDP - 1], compact.at[k - 1], m_sem + k - 1, dp_peer(k)))
 
-    sr_sem = take(NZ)
     xa_sem, xb_sem = take(NZ), take(NZ)
     nl_sem, nr_sem = take(NZ), take(NZ)
-    zr_sem = take(NZ - 1)
+    zr_sem = take(NZ)
     sent_r = []
 
     def stage_a(k):
-        zk = wrap(z + k + 1, NZ)
-        left_side = mine[...]
+        zk = z_at(NZ - 1 - k) if k < NZ - 1 else z
+        ours, other_side = mine[...], theirs[...]
 
         def one(x_, carry):
-            part[k, x_] = jnp.dot(
-                left_side, wt[at(other, x_, zk)], preferred_element_type=F32
-            ).astype(BF16)
+            kept[k, x_] = jnp.dot(ours, wt[at(c, x_, zk)], preferred_element_type=F32) + jnp.dot(
+                other_side, wsib[x_ * NZ + zk], preferred_element_type=F32
+            )
             return carry
 
         lax.fori_loop(0, NX, one, 0)
-        rows = pl.ds(0, REAL)
-        sent_r.append(send(part.at[k, :, rows], sib_in.at[k, :, rows], sr_sem + k, sibling))
-
-        def two(x_, carry):
-            kept[k, x_] = jnp.dot(left_side, wt[at(c, x_, zk)], preferred_element_type=F32)
-            return carry
-
-        lax.fori_loop(0, NX, two, 0)
 
     def pair(k, x_):
-        return kept[k, x_, :REAL] + sib_in[k, x_, :REAL].astype(F32)
+        return kept[k, x_, :REAL]
 
     def stage_b(k):
-        arrived(sib_in.at[k, :, pl.ds(0, REAL)], sr_sem + k)
         opp_out[k] = pair(k, xo).astype(BF16)
         if k in straight:
             sent_r.append(send(opp_out.at[k], opp_in.at[k // (NZ - 1)], xa_sem + k, opposite))
@@ -370,11 +368,11 @@
             value = value + opp_in[k // (NZ - 1)].astype(F32)
         if k < NZ - 1:
             z_out[k] = value.astype(BF16)
-            sent_r.append(send(z_out.at[k], z_in.at[k], zr_sem + k, z_peer(k + 1)))
+            sent_r.append(send(z_out.at[k], z_in.at[z], zr_sem + z, z_peer(NZ - 1 - k)))
         else:
             total[...] = value
 
-    qz_sem = take(NZ - 1)
+    qz_sem = take(NZ)
     ql_sem, qr_sem, qa_sem, qb_sem = take(NZ), take(NZ), take(NZ), take(NZ)
     qs_sem = take(NZ)
 
@@ -386,13 +384,13 @@
             arrived(extra.at[k - 1, c * NZ + z, quarter], q_sem + k - 1)
         piece = extra.at[:, c * NZ + z, quarter]
         for k in range(1, NZ):
-            sent_q.append(send(piece, piece, qz_sem + k - 1, z_peer(k)))
+            sent_q.append(send(piece, piece, qz_sem + z, z_peer(k)))
         sent_q.append(send(piece, piece, ql_sem + 0, right))
         sent_q.append(send(piece, piece, qr_sem + 0, left))
 
     def spread_2(k):
         piece = extra.at[:, c * NZ + z_at(k), quarter]
-        arrived(piece, qz_sem + k - 1)
+        arrived(piece, qz_sem + z_at(k))
         sent_q.append(send(piece, piece, ql_sem + k, right))
         sent_q.append(send(piece, piece, qr_sem + k, left))
 
@@ -412,16 +410,17 @@
         piece = extra.at[:, here]
         sent_q.append(send(piece, piece, qs_sem + k, sibling))
 
+    arrived(theirs, theirs_sem)
     stage_a(0)
-    stage_a(1)
     stage_b(0)
     stage_c(0)
+    stage_a(1)
+    stage_b(1)
     stage_a(2)
-    stage_b(1)
+    stage_b(2)
     spread_1()
+    stage_c(1)
     stage_a(3)
-    stage_b(2)
-    stage_c(1)
     stage_d(0)
     stage_c(2)
     stage_d(1)
@@ -435,17 +434,18 @@
     stage_d(3)
 
     value = total[...]
-    for k in range(NZ - 1):
-        arrived(z_in.at[k], zr_sem + k)
-        value = value + z_in[k].astype(F32)
+    for k in range(1, NZ):
+        arrived(z_in.at[z_at(k)], zr_sem + z_at(k))
+        value = value + z_in[z_at(k)].astype(F32)
     ret_out[...] = jnp.dot(
         unpack[:, :REAL], value.astype(BF16), preferred_element_type=F32
     ).astype(BF16)
 
     yr_sem = take(NY - 1)
+    sent_b = []
     for k in range(1, NY):
         there = pl.ds(pl.multiple_of(wrap(y + k, NY) * BLK, BLK), BLK)
-        sent_r.append(send(ret_out.at[there], ret.at[my_rows], yr_sem + k - 1, y_peer(k)))
+        sent_b.append(send(ret_out.at[there], ret.at[my_rows], yr_sem + k - 1, y_peer(k)))
     ret[my_rows, :] = ret_out[my_rows, :]
     spread_4(0)
     for k in range(1, NZ):
@@ -473,8 +473,9 @@
                 )
             gpart[z_ * NC + c_] = value
 
-    for copy in sent_y + sent_g:
+    for copy in sent_y + sent_g + sent_m + sent_r + sent_w:
         copy.wait_send()
+    arrived(chunk.at[other_at, own_rows], slots_sem)
     gradient(0)
     gradient(1)
     gradient(2)
@@ -482,13 +483,14 @@
     gate_of = jnp.where(first, pick * weight_of, 0.0)
     high = gate_of.astype(BF16)
     low_part = (gate_of - high.astype(F32)).astype(BF16)
+    back_to = jnp.concatenate([high, low_part, pick_cot], axis=1)
     for k in range(1, NY):
         from_y = pl.ds(pl.multiple_of(wrap(y + NY - k, NY) * BLK, BLK), BLK)
         arrived(ret.at[from_y], yr_sem + k - 1)
     got = ret[...]
-    out = tn_dot(got, high) + tn_dot(got, low_part)
-    mixed[...] = out[:cols].astype(BF16)
-    tgrad[...] = tn_dot(got, pick_cot)[:cols].astype(BF16)
+    out = tn_dot(got, back_to)[:cols]
+    mixed[...] = (out[:, :ROWS] + out[:, ROWS : 2 * ROWS]).astype(BF16)
+    tgrad[...] = out[:, 2 * ROWS :].astype(BF16)
 
     gradient(3)
     gbuf[...] = jnp.zeros_like(gbuf)
@@ -506,7 +508,7 @@
     ugrad[...] = gbuf[HID : 2 * HID].astype(BF16)
     dgrad[...] = gbuf[2 * HID :].astype(BF16)
 
-    for copy in sent_q + sent_m + sent_r:
+    for copy in sent_q + sent_b:
         copy.wait_send()
 
 
@@ -555,12 +557,14 @@
             pltpu.VMEM(chunk_of, BF16),
             pltpu.VMEM((CHUNKS,) + chunk_of, BF16),
             pltpu.VMEM(chunk_of, F32),
+            pltpu.VMEM(chunk_of, F32),
+            pltpu.VMEM(real_of, F32),
             pltpu.VMEM(chunk_of, BF16),
+            pltpu.VMEM(chunk_of, BF16),
+            pltpu.VMEM((NX * NZ, LANES, LANES), BF16),
             pltpu.VMEM((NDP, ROWS // 2, LANES), BF16),
             pltpu.VMEM((NDP - 1, NC * NZ) + chunk_of, BF16),
-            pltpu.VMEM((NZ, NX) + chunk_of, BF16),
             pltpu.VMEM((NZ, NX) + chunk_of, F32),
-            pltpu.VMEM((NZ, NX) + chunk_of, BF16),
             pltpu.VMEM((NZ,) + real_of, BF16),
             pltpu.VMEM((NZ, HALF, LANES), BF16),
             pltpu.VMEM((NZ, REAL - HALF, LANES), BF16),
@@ -570,7 +574,7 @@
             pltpu.VMEM((NZ,) + real_of, BF16),
             pltpu.VMEM((NZ,) + real_of, BF16),
             pltpu.VMEM((NZ - 1,) + real_of, BF16),
-            pltpu.VMEM((NZ - 1,) + real_of, BF16),
+            pltpu.VMEM((NZ,) + real_of, BF16),
             pltpu.VMEM(real_of, F32),
             pltpu.VMEM(chunk_of, BF16),
             pltpu.VMEM(chunk_of, BF16),

time: 72.6 us -> 71.7 us (0.988)
  Pallas kernels: 71.8 us -> 70.9 us
    pallas_call x1, Pallas kernels: 70.8 us -> 69.9 us  [per_device(): pl.pallas_call(kernel, out_shape=shapes, in_specs=[hbm] * 7, out_specs=[v...]
where the time goes in v3:
time: 71.7 us; the launch traced here: 71.5 us
  Pallas kernels  70.9 us (99%)
    pallas_call x1, Pallas kernels, per_device(): pl.pallas_call(kernel, out_shape=shapes, in_specs=[hbm] * 7, out_specs=[v...  69.9 us

profile of v3, /device:TPU:1, one launch (start us, length us, event | category | flops | bytes accessed | tf_op | source)
XLA Modules:
  0.0 71.5 jit_solution(13936167088133882491)
XLA Ops:
  0.6 69.9 %experts.1 = (bf16[224,128]{1,0:T(8,128)(2,1)S(1)}, bf16[224,128]{1,0:T(8,128)(2,1)S(1)}, bf16[64,1792]{1,0:T(8,128)(2,1)S(1)}, bf16[64,1792]{1,0:T(8,128)(2,1)S(1)}, bf16[64,1792]{1,0:T(8,128)(2,1)S(1)}) custom-call(bf16[224,128]{1,0:T(8,128)(2,1)} %bitcast.6, bf16[224,128]{1,0:T(8,128)(2,1)} %bitcast.7, s32[8,128]{1,0:T(8,128)} %bitcast.8, ...), custom_call_target="tpu_custom_call" | custom-call | tf_op jit(solution)/shard_map/experts/pallas_call | solution.py:544
  70.6 0.9 %write_out.1 = (bf16[224,128]{1,0:T(8,128)(2,1)}, bf16[224,128]{1,0:T(8,128)(2,1)}, bf16[64,1792]{1,0:T(8,128)(2,1)}, bf16[64,1792]{1,0:T(8,128)(2,1)}, bf16[64,1792]{1,0:T(8,128)(2,1)}) custom-call(bf16[224,128]{1,0:T(8,128)(2,1)S(1)} %get-tuple-element.15.refs_0_, bf16[224,128]{1,0:T(8,128)(2,1)S(1)} %get-tuple-element.16.refs_1_, ...), custom_call_target="tpu_custom_call" | custom-call | tf_op jit(solution)/shard_map/write_out/pallas_call | solution.py:591

commit v4 on v3

--- a/solution.py
+++ b/solution.py
@@ -191,7 +191,8 @@
     sent_g = []
     sent_q = []
     opposite = tensor_at(xo, z, c)
-    straight = (0, NZ - 1)
+    straight = (0, 3)
+    bend = (0, 1, 2, 3)
 
     def real(g, start=0, size=REAL):
         return chunk.at[g, pl.ds(start, size)]
@@ -335,15 +336,15 @@
 
     def stage_b(k):
         opp_out[k] = pair(k, xo).astype(BF16)
-        if k in straight:
-            sent_r.append(send(opp_out.at[k], opp_in.at[k // (NZ - 1)], xa_sem + k, opposite))
+        if k in bend:
+            sent_r.append(send(opp_out.at[k], opp_in.at[k], xa_sem + k, opposite))
             return
         sent_r.append(send(opp_out.at[k, pl.ds(0, HALF)], opp_a.at[k], xa_sem + k, right))
         sent_r.append(send(opp_out.at[k, pl.ds(HALF, REAL - HALF)], opp_b.at[k], xb_sem + k, left))
 
     def stage_c(k):
         value = pair(k, xr)
-        if k in straight:
+        if k in bend:
             right_out[k] = value.astype(BF16)
         else:
             arrived(opp_a.at[k], xa_sem + k)
@@ -351,7 +352,7 @@
             right_out[k, HALF:] = value[HALF:].astype(BF16)
         sent_r.append(send(right_out.at[k], from_left.at[k], nl_sem + k, right))
         value = pair(k, xl)
-        if k in straight:
+        if k in bend:
             left_out[k] = value.astype(BF16)
         else:
             arrived(opp_b.at[k], xb_sem + k)
@@ -363,9 +364,9 @@
         arrived(from_left.at[k], nl_sem + k)
         arrived(from_right.at[k], nr_sem + k)
         value = pair(k, x) + from_left[k].astype(F32) + from_right[k].astype(F32)
-        if k in straight:
-            arrived(opp_in.at[k // (NZ - 1)], xa_sem + k)
-            value = value + opp_in[k // (NZ - 1)].astype(F32)
+        if k in bend:
+            arrived(opp_in.at[k], xa_sem + k)
+            value = value + opp_in[k].astype(F32)
         if k < NZ - 1:
             z_out[k] = value.astype(BF16)
             sent_r.append(send(z_out.at[k], z_in.at[z], zr_sem + z, z_peer(NZ - 1 - k)))
@@ -386,27 +387,21 @@
         for k in range(1, NZ):
             sent_q.append(send(piece, piece, qz_sem + z, z_peer(k)))
         sent_q.append(send(piece, piece, ql_sem + 0, right))
+        sent_q.append(send(piece, piece, qa_sem + 0, opposite))
         sent_q.append(send(piece, piece, qr_sem + 0, left))
 
     def spread_2(k):
         piece = extra.at[:, c * NZ + z_at(k), quarter]
         arrived(piece, qz_sem + z_at(k))
         sent_q.append(send(piece, piece, ql_sem + k, right))
+        sent_q.append(send(piece, piece, qa_sem + k, opposite))
         sent_q.append(send(piece, piece, qr_sem + k, left))
 
-    def spread_3(k):
+    def spread_4(k):
         here = c * NZ + z_at(k)
         arrived(extra.at[:, here, part_rows(xl, 0, QUART)], ql_sem + k)
-        piece = extra.at[:, here, part_rows(xl, 0, QUART // 2)]
-        sent_q.append(send(piece, piece, qa_sem + k, right))
         arrived(extra.at[:, here, part_rows(xr, 0, QUART)], qr_sem + k)
-        piece = extra.at[:, here, part_rows(xr, QUART // 2, QUART // 2)]
-        sent_q.append(send(piece, piece, qb_sem + k, left))
-
-    def spread_4(k):
-        here = c * NZ + z_at(k)
-        arrived(extra.at[:, here, part_rows(xo, 0, QUART // 2)], qa_sem + k)
-        arrived(extra.at[:, here, part_rows(xo, QUART // 2, QUART // 2)], qb_sem + k)
+        arrived(extra.at[:, here, part_rows(xo, 0, QUART)], qa_sem + k)
         piece = extra.at[:, here]
         sent_q.append(send(piece, piece, qs_sem + k, sibling))
 
@@ -416,18 +411,17 @@
     stage_c(0)
     stage_a(1)
     stage_b(1)
+    stage_c(1)
     stage_a(2)
     stage_b(2)
+    stage_c(2)
     spread_1()
-    stage_c(1)
     stage_a(3)
-    stage_d(0)
-    stage_c(2)
-    stage_d(1)
-    spread_2(1)
     stage_b(3)
     stage_c(3)
-    spread_3(0)
+    stage_d(0)
+    spread_2(1)
+    stage_d(1)
     spread_2(2)
     spread_2(3)
     stage_d(2)
@@ -448,10 +442,9 @@
         sent_b.append(send(ret_out.at[there], ret.at[my_rows], yr_sem + k - 1, y_peer(k)))
     ret[my_rows, :] = ret_out[my_rows, :]
     spread_4(0)
-    for k in range(1, NZ):
-        spread_3(k)
-    for k in range(1, NZ):
-        spread_4(k)
+    spread_4(1)
+    spread_4(2)
+    spread_4(3)
 
     for k in range(1, NDP):
         arrived(compact.at[k - 1], m_sem + k - 1)
@@ -568,7 +561,7 @@
             pltpu.VMEM((NZ,) + real_of, BF16),
             pltpu.VMEM((NZ, HALF, LANES), BF16),
             pltpu.VMEM((NZ, REAL - HALF, LANES), BF16),
-            pltpu.VMEM((2,) + real_of, BF16),
+            pltpu.VMEM((NZ,) + real_of, BF16),
             pltpu.VMEM((NZ,) + real_of, BF16),
             pltpu.VMEM((NZ,) + real_of, BF16),
             pltpu.VMEM((NZ,) + real_of, BF16),

time: 71.7 us -> 71.9 us (level)
  no operation moved by 1% of the time
where the time goes in v4:
time: 71.9 us; the launch traced here: 71.8 us
  Pallas kernels  71.1 us (99%)
    pallas_call x1, Pallas kernels, per_device(): pl.pallas_call(kernel, out_shape=shapes, in_specs=[hbm] * 7, out_specs=[v...  70.2 us

profile of v4, /device:TPU:1, one launch (start us, length us, event | category | flops | bytes accessed | tf_op | source)
XLA Modules:
  0.0 71.8 jit_solution(18426349878395198474)
XLA Ops:
  0.6 70.2 %experts.1 = (bf16[224,128]{1,0:T(8,128)(2,1)S(1)}, bf16[224,128]{1,0:T(8,128)(2,1)S(1)}, bf16[64,1792]{1,0:T(8,128)(2,1)S(1)}, bf16[64,1792]{1,0:T(8,128)(2,1)S(1)}, bf16[64,1792]{1,0:T(8,128)(2,1)S(1)}) custom-call(bf16[224,128]{1,0:T(8,128)(2,1)} %bitcast.6, bf16[224,128]{1,0:T(8,128)(2,1)} %bitcast.7, s32[8,128]{1,0:T(8,128)} %bitcast.8, ...), custom_call_target="tpu_custom_call" | custom-call | tf_op jit(solution)/shard_map/experts/pallas_call | solution.py:537
  70.8 0.9 %write_out.1 = (bf16[224,128]{1,0:T(8,128)(2,1)}, bf16[224,128]{1,0:T(8,128)(2,1)}, bf16[64,1792]{1,0:T(8,128)(2,1)}, bf16[64,1792]{1,0:T(8,128)(2,1)}, bf16[64,1792]{1,0:T(8,128)(2,1)}) custom-call(bf16[224,128]{1,0:T(8,128)(2,1)S(1)} %get-tuple-element.15.refs_0_, bf16[224,128]{1,0:T(8,128)(2,1)S(1)} %get-tuple-element.16.refs_1_, ...), custom_call_target="tpu_custom_call" | custom-call | tf_op jit(solution)/shard_map/write_out/pallas_call | solution.py:584

commit v5 on v3

--- a/solution.py
+++ b/solution.py
@@ -191,7 +191,8 @@
     sent_g = []
     sent_q = []
     opposite = tensor_at(xo, z, c)
-    straight = (0, NZ - 1)
+    straight = (0, 3)
+    bend = (0, 3)
 
     def real(g, start=0, size=REAL):
         return chunk.at[g, pl.ds(start, size)]
@@ -305,9 +306,10 @@
     mine[...] = jnp.concatenate([top, bottom, tail], axis=0).astype(BF16)
 
     sent_w.append(send(mine, theirs, theirs_sem, sibling))
-    compact[NDP - 1] = jnp.concatenate(
-        [jnp.concatenate([deltas, hid], axis=1), pad], axis=0
-    ).astype(BF16)
+    wide_hid = jnp.concatenate([hid, jnp.zeros((ROWS // 2 - half_rows, 2 * HID), F32)], axis=0)
+    folded = wide_hid[: ROWS // 4] + pltpu.roll(wide_hid[ROWS // 4 :], HID, 1)
+    gap = jnp.zeros((ROWS // 2 - half_rows, 2 * HID), F32)
+    compact[NDP - 1] = jnp.concatenate([deltas, gap, folded], axis=0).astype(BF16)
     m_sem = take(NDP - 1)
     sent_m = []
     for k in range(1, NDP):
@@ -335,15 +337,15 @@
 
     def stage_b(k):
         opp_out[k] = pair(k, xo).astype(BF16)
-        if k in straight:
-            sent_r.append(send(opp_out.at[k], opp_in.at[k // (NZ - 1)], xa_sem + k, opposite))
+        if k in bend:
+            sent_r.append(send(opp_out.at[k], opp_in.at[k], xa_sem + k, opposite))
             return
         sent_r.append(send(opp_out.at[k, pl.ds(0, HALF)], opp_a.at[k], xa_sem + k, right))
         sent_r.append(send(opp_out.at[k, pl.ds(HALF, REAL - HALF)], opp_b.at[k], xb_sem + k, left))
 
     def stage_c(k):
         value = pair(k, xr)
-        if k in straight:
+        if k in bend:
             right_out[k] = value.astype(BF16)
         else:
             arrived(opp_a.at[k], xa_sem + k)
@@ -351,7 +353,7 @@
             right_out[k, HALF:] = value[HALF:].astype(BF16)
         sent_r.append(send(right_out.at[k], from_left.at[k], nl_sem + k, right))
         value = pair(k, xl)
-        if k in straight:
+        if k in bend:
             left_out[k] = value.astype(BF16)
         else:
             arrived(opp_b.at[k], xb_sem + k)
@@ -363,9 +365,9 @@
         arrived(from_left.at[k], nl_sem + k)
         arrived(from_right.at[k], nr_sem + k)
         value = pair(k, x) + from_left[k].astype(F32) + from_right[k].astype(F32)
-        if k in straight:
-            arrived(opp_in.at[k // (NZ - 1)], xa_sem + k)
-            value = value + opp_in[k // (NZ - 1)].astype(F32)
+        if k in bend:
+            arrived(opp_in.at[k], xa_sem + k)
+            value = value + opp_in[k].astype(F32)
         if k < NZ - 1:
             z_out[k] = value.astype(BF16)
             sent_r.append(send(z_out.at[k], z_in.at[z], zr_sem + z, z_peer(NZ - 1 - k)))
@@ -457,9 +459,11 @@
         arrived(compact.at[k - 1], m_sem + k - 1)
     sides = []
     for k in range(NDP):
-        both = compact[k, :half_rows].astype(F32)
-        top = jnp.concatenate([both[:, : 2 * HID], zeros], axis=1)
-        bottom = jnp.concatenate([zeros, both[:, 2 * HID :]], axis=1)
+        both = compact[k].astype(F32)
+        folded = both[ROWS // 2 :]
+        unfolded = jnp.concatenate([folded, pltpu.roll(folded, HID, 1)], axis=0)[:half_rows]
+        top = jnp.concatenate([both[:half_rows], zeros], axis=1)
+        bottom = jnp.concatenate([zeros, jnp.where(low, unfolded, 0.0)], axis=1)
         side = jnp.concatenate([top, bottom, tail], axis=0)
         sides.append(jnp.transpose(side)[: 3 * HID].astype(BF16))
     def gradient(k):
@@ -562,13 +566,13 @@
             pltpu.VMEM(chunk_of, BF16),
             pltpu.VMEM(chunk_of, BF16),
             pltpu.VMEM((NX * NZ, LANES, LANES), BF16),
-            pltpu.VMEM((NDP, ROWS // 2, LANES), BF16),
+            pltpu.VMEM((NDP, 3 * ROWS // 4, LANES // 2), BF16),
             pltpu.VMEM((NDP - 1, NC * NZ) + chunk_of, BF16),
             pltpu.VMEM((NZ, NX) + chunk_of, F32),
             pltpu.VMEM((NZ,) + real_of, BF16),
             pltpu.VMEM((NZ, HALF, LANES), BF16),
             pltpu.VMEM((NZ, REAL - HALF, LANES), BF16),
-            pltpu.VMEM((2,) + real_of, BF16),
+            pltpu.VMEM((NZ,) + real_of, BF16),
             pltpu.VMEM((NZ,) + real_of, BF16),
             pltpu.VMEM((NZ,) + real_of, BF16),
             pltpu.VMEM((NZ,) + real_of, BF16),

time: 71.7 us -> 71.8 us (level)
  no operation moved by 1% of the time
where the time goes in v5:
time: 71.8 us; the launch traced here: 71.6 us
  Pallas kernels  71 us (99%)
    pallas_call x1, Pallas kernels, per_device(): pl.pallas_call(kernel, out_shape=shapes, in_specs=[hbm] * 7, out_specs=[v...  70 us

profile of v5, /device:TPU:1, one launch (start us, length us, event | category | flops | bytes accessed | tf_op | source)
XLA Modules:
  0.0 71.6 jit_solution(4303818615614780500)
XLA Ops:
  0.6 70.0 %experts.1 = (bf16[224,128]{1,0:T(8,128)(2,1)S(1)}, bf16[224,128]{1,0:T(8,128)(2,1)S(1)}, bf16[64,1792]{1,0:T(8,128)(2,1)S(1)}, bf16[64,1792]{1,0:T(8,128)(2,1)S(1)}, bf16[64,1792]{1,0:T(8,128)(2,1)S(1)}) custom-call(bf16[224,128]{1,0:T(8,128)(2,1)} %bitcast.6, bf16[224,128]{1,0:T(8,128)(2,1)} %bitcast.7, s32[8,128]{1,0:T(8,128)} %bitcast.8, ...), custom_call_target="tpu_custom_call" | custom-call | tf_op jit(solution)/shard_map/experts/pallas_call | solution.py:548
  70.7 0.9 %write_out.1 = (bf16[224,128]{1,0:T(8,128)(2,1)}, bf16[224,128]{1,0:T(8,128)(2,1)}, bf16[64,1792]{1,0:T(8,128)(2,1)}, bf16[64,1792]{1,0:T(8,128)(2,1)}, bf16[64,1792]{1,0:T(8,128)(2,1)}) custom-call(bf16[224,128]{1,0:T(8,128)(2,1)S(1)} %get-tuple-element.15.refs_0_, bf16[224,128]{1,0:T(8,128)(2,1)S(1)} %get-tuple-element.16.refs_1_, ...), custom_call_target="tpu_custom_call" | custom-call | tf_op jit(solution)/shard_map/write_out/pallas_call | solution.py:595
